TPU v7x, 256 devices: a whole 4x4x8 slice. The times are simulated.
256 devices in a mesh: tm: 64 (over z, x, core), depth: 4 (over y).
Axes of the slice: x: 4, y: 4, z: 8, core: 2. Of those that a mesh axis runs over, the one named last changes fastest.
Arguments:
- iq: bfloat16 [2, 384, 192, 512], P(None, 'tm', 'depth')
- half: int32 [192], P('depth'), may hold values from 1 to 8, as said below
- weights: int32 [6], replicated, may hold values from 1 to 4
Outputs:
- displacement: float32 [384, 192, 512], P('tm', 'depth')
Inputs may be any that keep to these rules, and one draw needn't show every extreme that they name: `half`: every value is reached at some depth.
All inputs are finite; a program needn't handle non-finite values.
Results may differ from a plain program's by a relative error of at most 0.00035.
Values may be sent and summed in bfloat16 or wider, within the bound.
A program may use at most 64 MiB of HBM per device.

v0:
```python
import jax
import jax.numpy as jnp
from jax import lax
from jax.sharding import PartitionSpec as P

LAGS = 6
HMAX = 8


def extended_2(block, sides, width):
    for axis, dim in sides:
        count = lax.axis_size(axis)
        forward = [(i, i + 1) for i in range(count - 1)]
        backward = [(target, source) for source, target in forward]
        low = lax.ppermute(
            lax.slice_in_dim(block, block.shape[dim] - width, None, axis=dim), axis, forward
        )
        high = lax.ppermute(lax.slice_in_dim(block, 0, width, axis=dim), axis, backward)
        block = jnp.concatenate([low, block, high], axis=dim)
    return block


def from_behind(array, axis, by):
    peers = lax.axis_size(axis)
    pairs = [(i, i + by) for i in range(peers) if 0 <= i + by < peers]
    return lax.ppermute(array, axis, pairs)


def window(padded, half):
    depth_count = half.shape[0]
    total = jnp.zeros(padded.shape[:1] + (depth_count,) + padded.shape[2:], jnp.float32)
    for offset in range(-HMAX, HMAX + 1):
        keep = (jnp.abs(offset) <= half)[:, None]
        total = total + jnp.where(
            keep, padded[:, HMAX + offset : HMAX + offset + depth_count], jnp.float32(0.0)
        )
    return total


def pair_phase(later, earlier, half):
    later = later.astype(jnp.float32)
    earlier = earlier.astype(jnp.float32)
    real_part = later[0] * earlier[0] + later[1] * earlier[1]
    imag_part = later[1] * earlier[0] - later[0] * earlier[1]
    return jnp.arctan2(window(imag_part, half), window(real_part, half))


def front_pad(values, before, after):
    return jnp.pad(values, ((before, after), (0, 0), (0, 0)))


def shards(iq, half, weights):
    frame_count = iq.shape[1]
    depth_count = iq.shape[2]
    line_count = iq.shape[3]
    total_frames = frame_count * lax.axis_size("tm")
    first = lax.axis_index("tm") * frame_count
    frame_ids = jnp.arange(frame_count, dtype=jnp.int32) + first
    padded = extended_2(iq, (("depth", 2),), HMAX)
    head = from_behind(padded, "tm", -1)
    numer = jnp.zeros((frame_count, depth_count, line_count), jnp.float32)
    denom = jnp.zeros((frame_count,), jnp.float32)
    for lag in range(1, LAGS + 1):
        weight = weights[lag - 1].astype(jnp.float32)
        denom = denom + weight * (
            (frame_ids + lag < total_frames).astype(jnp.float32)
            + (frame_ids - lag >= 0).astype(jnp.float32)
        )
    extended = jnp.concatenate([padded, head], axis=1)
    tails = []
    for lag in range(1, LAGS + 1):
        weight = weights[lag - 1].astype(jnp.float32)
        phase = pair_phase(extended[:, lag : lag + frame_count], extended[:, :frame_count], half)
        valid = (frame_ids + lag < total_frames)[:, None, None]
        numer = numer + weight * jnp.where(valid, phase, jnp.float32(0.0))
        numer = numer + weight * front_pad(phase[: frame_count - lag], lag, 0)
        tails.append(phase[frame_count - lag :])
    moved = from_behind(jnp.concatenate(tails, axis=0), "tm", 1)
    position = 0
    for lag in range(1, LAGS + 1):
        weight = weights[lag - 1].astype(jnp.float32)
        numer = numer + weight * front_pad(moved[position : position + lag], 0, frame_count - lag)
        position = position + lag
    return numer / denom[:, None, None]


def solution(mesh):
    placed = (P(None, "tm", "depth", None), P("depth"), P())
    return jax.shard_map(
        shards, mesh=mesh, in_specs=placed, out_specs=P("tm", "depth", None), check_vma=False
    )
```

profile of v0, /device:TPU:128, one launch (start us, length us, event | category | flops | bytes accessed | tf_op | source)
XLA Modules:
  0.0 93.5 jit_solution(7637725152978779151)
XLA Ops:
  0.0 1.0 %fusion.243 = (bf16[2,6,8,512]{3,2,1,0:T(8,128)(2,1)S(1)}, bf16[2,6,8,512]{3,2,1,0:T(8,128)(2,1)S(1)}) fusion(bf16[2,6,48,512]{3,2,1,0:T(8,128)(2,1)} %param.3), kind=kLoop, calls=%fused_computation.501 | loop fusion | bytes 393216 | tf_op jit(solution)/shard_map/slice | solution.py:18
  1.0 3.5 %collective-permute-start = (bf16[2,6,8,512]{3,2,1,0:T(8,128)(2,1)S(1)}, bf16[2,6,8,512]{3,2,1,0:T(8,128)(2,1)S(1)}, u32[]{:S(2)}, u32[]{:S(2)}) collective-permute-start(bf16[2,6,8,512]{3,2,1,0:T(8,128)(2,1)S(1)} %get-tuple-element.35), channel_id=1, source_target_pairs={{0,1},{1,2},{2,3},{4,5},{5,6},{6,7},{8,9},{9,10},{10,11},{12,13},{... | collective-permute-start | bytes 294920 | tf_op jit(solution)/shard_map/ppermute | solution.py:15
  4.5 1.3 %collective-permute-start.1 = (bf16[2,6,8,512]{3,2,1,0:T(8,128)(2,1)S(1)}, bf16[2,6,8,512]{3,2,1,0:T(8,128)(2,1)S(1)}, u32[]{:S(2)}, u32[]{:S(2)}) collective-permute-start(bf16[2,6,8,512]{3,2,1,0:T(8,128)(2,1)S(1)} %get-tuple-element.34), channel_id=1, source_target_pairs={{1,0},{2,1},{3,2},{5,4},{6,5},{7,6},{9,8},{10,9},{11,10},{13,12},{... | collective-permute-start | bytes 294920 | tf_op jit(solution)/shard_map/ppermute | solution.py:18
  5.8 0.9 collective-permute-done
  6.7 1.1 %constant_dynamic-update-slice_fusion.1 = bf16[2,6,64,512]{3,2,1,0:T(8,128)(2,1)S(1)} fusion(bf16[2,6,64,512]{3,2,1,0:T(8,128)(2,1)S(1)} %constant_dynamic-update-slice_fusion.2, bf16[2,6,48,512]{3,2,1,0:T(8,128)(2,1)} %param.3), kind=kLoop, calls=%fused_computation.458 | loop fusion | bytes 1179648
  7.8 3.2 %collective-permute-done.1 = bf16[2,6,8,512]{3,2,1,0:T(8,128)(2,1)S(1)} collective-permute-done((bf16[2,6,8,512]{3,2,1,0:T(8,128)(2,1)S(1)}, bf16[2,6,8,512]{3,2,1,0:T(8,128)(2,1)S(1)}, u32[]{:S(2)}, u32[]{:S(2)}) %collective-permute-start.1) | collective-permute-done | bytes 98336 | tf_op jit(solution)/shard_map/ppermute | solution.py:18
  11.0 2.2 %collective-permute-start.2 = (bf16[2,6,64,512]{3,2,1,0:T(8,128)(2,1)S(1)}, bf16[2,6,64,512]{3,2,1,0:T(8,128)(2,1)S(1)}, u32[]{:S(2)}, u32[]{:S(2)}) collective-permute-start(bf16[2,6,64,512]{3,2,1,0:T(8,128)(2,1)S(1)} %constant_dynamic-update-slice_fusion), channel_id=1, source_target_pairs={{4,0},{8,4},{12,8},{16,12},{20,16},{24,20},{28,24},{32,28},{36,32}... | collective-permute-start | bytes 2359304 | tf_op jit(solution)/shard_map/ppermute | solution.py:26
  13.2 0.0 copy-done.10
  13.2 9.5 %collective-permute-done.2 = bf16[2,6,64,512]{3,2,1,0:T(8,128)(2,1)S(1)} collective-permute-done((bf16[2,6,64,512]{3,2,1,0:T(8,128)(2,1)S(1)}, bf16[2,6,64,512]{3,2,1,0:T(8,128)(2,1)S(1)}, u32[]{:S(2)}, u32[]{:S(2)}) %collective-permute-start.2) | collective-permute-done | bytes 786464 | tf_op jit(solution)/shard_map/ppermute | solution.py:26
  22.7 1.4 %fusion.8 = (f32[2,6,64,512]{3,2,1,0:T(8,128)S(1)}, f32[2,6,64,512]{3,2,1,0:T(8,128)S(1)}, f32[2,6,64,512]{3,2,1,0:T(8,128)S(1)}, f32[2,6,64,512]{3,2,1,0:T(8,12...) fusion(bf16[2,6,64,512]{3,2,1,0:T(8,128)(2,1)S(1)} %collective-permute-done.2, ...), kind=kLoop, calls=%fused_computation.17 | loop fusion | flops 4718592 | bytes 12582912 | tf_op jit(solution)/shard_map/convert_element_type | solution.py:41
  24.1 0.6 subtract_bitcast_fusion.2
  24.7 4.1 %fusion.183 = f32[6,48,512]{2,1,0:T(8,128)S(1)} fusion(f32[6,64,512]{2,1,0:T(8,128)S(1)} %get-tuple-element.28, f32[6,64,512]{2,1,0:T(8,128)S(1)} %get-tuple-element.29, pred[48]{0:T(512)(128)(4,1)S(1)} %get-tuple-element.49, pred[48]{0:T(512)(128)(4,1)S(1)} %get-tuple-element.50, pred[48]{0:T(512)(128)(4,1)S(1)} %get-tuple-element.43, ...), kind=kLoop, calls=%fused_computation.377 | loop fusion | flops 9732096 | bytes 20644272 | tf_op jit(solution)/shard_map/atan2 | solution.py:45
  28.8 0.0 copy-start.4
  28.8 0.7 slice_dynamic-update-slice_fusion.4
  29.5 0.7 subtract_bitcast_fusion.1
  30.2 4.1 %fusion.51 = f32[6,48,512]{2,1,0:T(8,128)S(1)} fusion(f32[6,64,512]{2,1,0:T(8,128)S(1)} %get-tuple-element.10, f32[6,64,512]{2,1,0:T(8,128)S(1)} %get-tuple-element.9, pred[48]{0:T(512)(128)(4,1)S(1)} %get-tuple-element.49, pred[48]{0:T(512)(128)(4,1)S(1)} %get-tuple-element.50, pred[48]{0:T(512)(128)(4,1)S(1)} %get-tuple-element.43, ...), kind=kLoop, calls=%fused_computation.109 | loop fusion | flops 9732096 | bytes 20644272 | tf_op jit(solution)/shard_map/atan2 | solution.py:45
  34.3 0.0 copy-start.5
  34.3 4.1 %fusion.84 = f32[6,48,512]{2,1,0:T(8,128)S(1)} fusion(f32[6,64,512]{2,1,0:T(8,128)S(1)} %get-tuple-element.12, f32[6,64,512]{2,1,0:T(8,128)S(1)} %get-tuple-element.11, pred[48]{0:T(512)(128)(4,1)S(1)} %get-tuple-element.49, pred[48]{0:T(512)(128)(4,1)S(1)} %get-tuple-element.50, pred[48]{0:T(512)(128)(4,1)S(1)} %get-tuple-element.43, ...), kind=kLoop, calls=%fused_computation.176 | loop fusion | flops 9732096 | bytes 20644272 | tf_op jit(solution)/shard_map/atan2 | solution.py:45
  38.4 0.0 copy-start
  38.4 0.7 subtract_bitcast_fusion
  39.1 4.1 %fusion.150 = f32[6,48,512]{2,1,0:T(8,128)S(1)} fusion(f32[6,64,512]{2,1,0:T(8,128)S(1)} %get-tuple-element.19, f32[6,64,512]{2,1,0:T(8,128)S(1)} %get-tuple-element.20, pred[48]{0:T(512)(128)(4,1)S(1)} %get-tuple-element.49, pred[48]{0:T(512)(128)(4,1)S(1)} %get-tuple-element.50, pred[48]{0:T(512)(128)(4,1)S(1)} %get-tuple-element.43, ...), kind=kLoop, calls=%fused_computation.310 | loop fusion | flops 9732096 | bytes 20644272 | tf_op jit(solution)/shard_map/atan2 | solution.py:45
  43.2 0.0 copy-start.2
  43.2 0.7 slice_dynamic-update-slice_fusion.3
  43.9 4.0 %fusion.117 = f32[6,48,512]{2,1,0:T(8,128)S(1)} fusion(f32[6,64,512]{2,1,0:T(8,128)S(1)} %get-tuple-element.21, f32[6,64,512]{2,1,0:T(8,128)S(1)} %get-tuple-element.22, pred[48]{0:T(512)(128)(4,1)S(1)} %get-tuple-element.49, pred[48]{0:T(512)(128)(4,1)S(1)} %get-tuple-element.50, pred[48]{0:T(512)(128)(4,1)S(1)} %get-tuple-element.43, ...), kind=kLoop, calls=%fused_computation.243 | loop fusion | flops 9732096 | bytes 20644272 | tf_op jit(solution)/shard_map/atan2 | solution.py:45
  48.0 0.9 fusion.242
  48.9 0.8 slice_dynamic-update-slice_fusion.1
  49.6 0.8 slice_dynamic-update-slice_fusion
  50.5 4.8 %constant_dynamic-update-slice_fusion.3 = (f32[21,48,512]{2,1,0:T(8,128)}, f32[6,48,512]{2,1,0:T(8,128)S(1)}) fusion(f32[21,48,512]{2,1,0:T(8,128)} %slice_dynamic-update-slice_fusion, f32[6,64,512]{2,1,0:T(8,128)S(1)} %get-tuple-element.8, f32[6,64,512]{2,1,0:T(8,128)S(1)} %get-tuple-element.7, pred[48]{0:T(512)(128)(4,1)S(1)} %get-tuple-element.49, ...), kind=kLoop, calls=%fused_computation.460 | loop fusion | flops 9732096 | bytes 21234096 | tf_op jit(solution)/shard_map/concatenate | solution.py:78
  55.2 3.4 %collective-permute-start.3 = (f32[21,48,512]{2,1,0:T(8,128)}, f32[21,48,512]{2,1,0:T(8,128)}, u32[]{:S(2)}, u32[]{:S(2)}) collective-permute-start(f32[21,48,512]{2,1,0:T(8,128)} %get-tuple-element.5), channel_id=1, source_target_pairs={{0,4},{4,8},{8,12},{12,16},{16,20},{20,24},{24,28},{28,32},{32,36}... | collective-permute-start | bytes 6193160 | tf_op jit(solution)/shard_map/ppermute | solution.py:26
  58.6 0.0 copy-done.8
  58.6 0.7 fusion.244
  63.1 0.0 copy-done.5
  63.1 0.0 copy-done
  63.1 0.0 copy-done.2
  63.1 0.0 copy-done.4
  63.1 0.0 copy-start.6
  63.1 0.0 copy-start.1
  63.1 0.0 slice-start
  63.2 0.0 slice-start.1
  63.2 0.0 slice-start.2
  63.2 0.0 slice-start.3
  63.2 0.0 copy-start.9
  63.2 22.8 %collective-permute-done.3 = f32[21,48,512]{2,1,0:T(8,128)} collective-permute-done((f32[21,48,512]{2,1,0:T(8,128)}, f32[21,48,512]{2,1,0:T(8,128)}, u32[]{:S(2)}, u32[]{:S(2)}) %collective-permute-start.3) | collective-permute-done | bytes 2064416 | tf_op jit(solution)/shard_map/ppermute | solution.py:26
  86.0 1.1 %slice.1275 = f32[5,48,512]{2,1,0:T(8,128)S(1)} slice(f32[21,48,512]{2,1,0:T(8,128)} %collective-permute-done.3), slice={[10:15], [0:48], [0:512]} | slice | bytes 983040 | tf_op jit(solution)/shard_map/slice | solution.py:82
  87.1 1.0 %slice.1274 = f32[4,48,512]{2,1,0:T(8,128)S(1)} slice(f32[21,48,512]{2,1,0:T(8,128)} %collective-permute-done.3), slice={[6:10], [0:48], [0:512]} | slice | bytes 786432 | tf_op jit(solution)/shard_map/slice | solution.py:82
  88.1 1.0 %slice.1273 = f32[3,48,512]{2,1,0:T(8,128)S(1)} slice(f32[21,48,512]{2,1,0:T(8,128)} %collective-permute-done.3), slice={[3:6], [0:48], [0:512]} | slice | bytes 589824 | tf_op jit(solution)/shard_map/slice | solution.py:82
  89.1 0.9 %slice.1272 = f32[2,48,512]{2,1,0:T(8,128)S(1)} slice(f32[21,48,512]{2,1,0:T(8,128)} %collective-permute-done.3), slice={[1:3], [0:48], [0:512]} | slice | bytes 393216 | tf_op jit(solution)/shard_map/slice | solution.py:82
  90.1 3.3 %fusion.10 = f32[6,48,512]{2,1,0:T(8,128)} fusion(f32[21,48,512]{2,1,0:T(8,128)} %collective-permute-done.3, f32[5,48,512]{2,1,0:T(8,128)S(1)} %slice.1275, f32[4,48,512]{2,1,0:T(8,128)S(1)} %slice.1274, f32[3,48,512]{2,1,0:T(8,128)S(1)} %slice.1273, f32[2,48,512]{2,1,0:T(8,128)S(1)} %slice.1272, f32[6,48,512]{2,1,0:T(8,128)S(1)} %get-tuple-element.6, ...), kind=kLoop, calls=%fused_computation.32 | loop fusion | flops 6045696 | bytes 8159326 | tf_op jit(solution)/shard_map/div | solution.py:84
  (20 shorter events, 0.1 us)
Async XLA Ops:
  0.0 13.2 %copy-start.10 = (s32[48]{0:T(128)S(1)}, s32[48]{0:T(128)}, u32[]{:S(2)}) copy-start(s32[48]{0:T(128)} %param.4) | copy-start | bytes 580
  1.0 5.7 %collective-permute-start = (bf16[2,6,8,512]{3,2,1,0:T(8,128)(2,1)S(1)}, bf16[2,6,8,512]{3,2,1,0:T(8,128)(2,1)S(1)}, u32[]{:S(2)}, u32[]{:S(2)}) collective-permute-start(bf16[2,6,8,512]{3,2,1,0:T(8,128)(2,1)S(1)} %get-tuple-element.35), channel_id=1, source_target_pairs={{0,1},{1,2},{2,3},{4,5},{5,6},{6,7},{8,9},{9,10},{10,11},{12,13},{... | collective-permute-start | bytes 294920 | tf_op jit(solution)/shard_map/ppermute | solution.py:15
  4.5 6.5 %collective-permute-start.1 = (bf16[2,6,8,512]{3,2,1,0:T(8,128)(2,1)S(1)}, bf16[2,6,8,512]{3,2,1,0:T(8,128)(2,1)S(1)}, u32[]{:S(2)}, u32[]{:S(2)}) collective-permute-start(bf16[2,6,8,512]{3,2,1,0:T(8,128)(2,1)S(1)} %get-tuple-element.34), channel_id=1, source_target_pairs={{1,0},{2,1},{3,2},{5,4},{6,5},{7,6},{9,8},{10,9},{11,10},{13,12},{... | collective-permute-start | bytes 294920 | tf_op jit(solution)/shard_map/ppermute | solution.py:18
  11.0 11.7 %collective-permute-start.2 = (bf16[2,6,64,512]{3,2,1,0:T(8,128)(2,1)S(1)}, bf16[2,6,64,512]{3,2,1,0:T(8,128)(2,1)S(1)}, u32[]{:S(2)}, u32[]{:S(2)}) collective-permute-start(bf16[2,6,64,512]{3,2,1,0:T(8,128)(2,1)S(1)} %constant_dynamic-update-slice_fusion), channel_id=1, source_target_pairs={{4,0},{8,4},{12,8},{16,12},{20,16},{24,20},{28,24},{32,28},{36,32}... | collective-permute-start | bytes 2359304 | tf_op jit(solution)/shard_map/ppermute | solution.py:26
  28.8 34.3 %copy-start.4 = (f32[6,48,512]{2,1,0:T(8,128)}, f32[6,48,512]{2,1,0:T(8,128)S(1)}, u32[]{:S(2)}) copy-start(f32[6,48,512]{2,1,0:T(8,128)S(1)} %fusion.183) | copy-start | bytes 1769476
  34.3 28.8 %copy-start.5 = (f32[6,48,512]{2,1,0:T(8,128)}, f32[6,48,512]{2,1,0:T(8,128)S(1)}, u32[]{:S(2)}) copy-start(f32[6,48,512]{2,1,0:T(8,128)S(1)} %fusion.51) | copy-start | bytes 1769476
  38.4 24.7 %copy-start = (f32[6,48,512]{2,1,0:T(8,128)}, f32[6,48,512]{2,1,0:T(8,128)S(1)}, u32[]{:S(2)}) copy-start(f32[6,48,512]{2,1,0:T(8,128)S(1)} %fusion.84) | copy-start | bytes 1769476
  43.2 19.9 %copy-start.2 = (f32[6,48,512]{2,1,0:T(8,128)}, f32[6,48,512]{2,1,0:T(8,128)S(1)}, u32[]{:S(2)}) copy-start(f32[6,48,512]{2,1,0:T(8,128)S(1)} %fusion.150) | copy-start | bytes 1769476
  50.5 8.1 %copy-start.8 = (s32[6]{0:T(128)S(1)}, s32[6]{0:T(128)}, u32[]{:S(2)}) copy-start(s32[6]{0:T(128)} %param.5) | copy-start | bytes 76
  55.2 30.8 %collective-permute-start.3 = (f32[21,48,512]{2,1,0:T(8,128)}, f32[21,48,512]{2,1,0:T(8,128)}, u32[]{:S(2)}, u32[]{:S(2)}) collective-permute-start(f32[21,48,512]{2,1,0:T(8,128)} %get-tuple-element.5), channel_id=1, source_target_pairs={{0,4},{4,8},{8,12},{12,16},{16,20},{20,24},{24,28},{28,32},{32,36}... | collective-permute-start | bytes 6193160 | tf_op jit(solution)/shard_map/ppermute | solution.py:26
  63.1 26.9 %copy-start.6 = (f32[6,48,512]{2,1,0:T(8,128)S(1)}, f32[6,48,512]{2,1,0:T(8,128)}, u32[]{:S(2)}) copy-start(f32[6,48,512]{2,1,0:T(8,128)} %copy-done.5) | copy-start | bytes 1769476
  63.1 26.9 %copy-start.1 = (f32[6,48,512]{2,1,0:T(8,128)S(1)}, f32[6,48,512]{2,1,0:T(8,128)}, u32[]{:S(2)}) copy-start(f32[6,48,512]{2,1,0:T(8,128)} %copy-done) | copy-start | bytes 1769476
  63.1 26.9 %slice-start = ((f32[6,48,512]{2,1,0:T(8,128)}), f32[2,48,512]{2,1,0:T(8,128)S(1)}, s32[]{:S(2)}) async-start(f32[6,48,512]{2,1,0:T(8,128)} %copy-done), calls=%async_computation | async-start | bytes 393216 | tf_op jit(solution)/shard_map/slice | solution.py:76
  63.2 26.9 %copy-start.3 = (f32[6,48,512]{2,1,0:T(8,128)S(1)}, f32[6,48,512]{2,1,0:T(8,128)}, u32[]{:S(2)}) copy-start(f32[6,48,512]{2,1,0:T(8,128)} %copy-done.2) | copy-start | bytes 1769476
  63.2 26.9 %slice-start.1 = ((f32[6,48,512]{2,1,0:T(8,128)}), f32[4,48,512]{2,1,0:T(8,128)S(1)}, s32[]{:S(2)}) async-start(f32[6,48,512]{2,1,0:T(8,128)} %copy-done.2), calls=%async_computation.1 | async-start | bytes 786432 | tf_op jit(solution)/shard_map/slice | solution.py:76
  63.2 26.9 %slice-start.2 = ((f32[6,48,512]{2,1,0:T(8,128)}), f32[5,48,512]{2,1,0:T(8,128)S(1)}, s32[]{:S(2)}) async-start(f32[6,48,512]{2,1,0:T(8,128)} %copy-done.4), calls=%async_computation.2 | async-start | bytes 983040 | tf_op jit(solution)/shard_map/slice | solution.py:76
  63.2 26.9 %slice-start.3 = ((f32[6,48,512]{2,1,0:T(8,128)}), f32[1,48,512]{2,1,0:T(8,128)S(1)}, s32[]{:S(2)}) async-start(f32[6,48,512]{2,1,0:T(8,128)} %copy-done.5), calls=%async_computation.3 | async-start | bytes 196608 | tf_op jit(solution)/shard_map/slice | solution.py:76
  63.2 26.9 %copy-start.7 = (f32[3,48,512]{2,1,0:T(8,128)S(1)}, f32[3,48,512]{2,1,0:T(8,128)}, u32[]{:S(2)}) copy-start(f32[3,48,512]{2,1,0:T(8,128)} %get-tuple-element.32) | copy-start | bytes 884740
  63.2 26.9 %copy-start.9 = (pred[6]{0:T(512)(128)(4,1)S(1)}, pred[6]{0:T(512)(128)(4,1)}, u32[]{:S(2)}) copy-start(pred[6]{0:T(512)(128)(4,1)} %constant.46.clone.1) | copy-start | bytes 22
where the time goes:
time: 93.9 us; the launch traced here: 93.5 us
  waiting for transfers between devices  36.3 us (39%)
  other arithmetic  31.8 us (34%)
  local copies, waits for them, and re-layouts  10.8 us (12%)
  starting transfers between devices  10.4 us (11%)
  between operations  4.15 us (4%)
    ppermute x2, waiting for transfers between devices, from_behind(): return lax.ppermute(array, axis, pairs)  32.3 us
    atan2 x5, other arithmetic, pair_phase(): return jnp.arctan2(window(imag_part, half), window(real_part, half))  20.3 us
    ppermute x2, starting transfers between devices, from_behind(): return lax.ppermute(array, axis, pairs)  5.59 us
    concatenate x1, other arithmetic, shards(): moved = from_behind(jnp.concatenate(tails, axis=0), 'tm', 1)  4.75 us
    unnamed x28, local copies, waits for them, and re-layouts  4.22 us
    slice x4, local copies, waits for them, and re-layouts, shards(): moved[position:position + lag]  4.01 us
    ppermute x1, starting transfers between devices, extended_2(): lax.ppermute(lax.slice_in_dim(block, block.shape[dim] - width, None, axis...  3.49 us
    div x1, other arithmetic, shards(): return numer / denom[:, None, None]  3.33 us
  transfers between devices with their start and end apart: 4, of which 4 were waited for; matrix products, arithmetic and copies ran while one was open for 2% of the time, Pallas kernels for 0%

commit v1 on v0

v1 whole, which is shorter than its diff:
```python
import functools

import jax
import jax.numpy as jnp
import numpy as np
from jax import lax
from jax.experimental import pallas as pl
from jax.experimental.pallas import tpu as pltpu
from jax.sharding import PartitionSpec as P

LAGS = 6
HMAX = 8
HALF_PI = float(np.float32(np.pi / 2))
PI = float(np.float32(np.pi))
TINY = 1.1754944e-38
ATAN = (
    0.9999960660934448,
    -0.33301785588264465,
    0.19582265615463257,
    -0.12176322191953659,
    0.05807745084166527,
    -0.0137208616361022,
)
MESH = pl.DeviceIdType.MESH
UNITS = 6
STEPS = 12
HEAD = 4
EDGE_STEPS = 7


def at_least(value, bound):
    return (value >= bound).astype(jnp.int32)


def signed_phase(y, x, weight):
    ax = jnp.abs(x)
    ay = jnp.abs(y)
    high = jnp.maximum(jnp.maximum(ax, ay), TINY)
    t = jnp.minimum(ax, ay) * pltpu.reciprocal(high, approx=True)
    s = t * t
    poly = ATAN[-1] * s + ATAN[-2]
    for coefficient in ATAN[-3::-1]:
        poly = poly * s + coefficient
    angle = poly * t
    angle = jnp.where(ay > ax, HALF_PI - angle, angle)
    angle = jnp.where(x < 0, PI - angle, angle)
    return angle * jnp.where(y < 0, -weight, weight)


def kernel(
    iq_any, half, weights, out,
    own16, edge_out, edge_in, near16, near_edge, field, total, sums, band, back,
    load_sem, edge_send, edge_recv, near_send, near_recv, far_send, far_recv, back_send, back_recv,
):
    frames, depth, lines = own16.shape[1:]
    strip = lines // 2
    rows = depth + 2 * HMAX
    me, level = lax.axis_index("tm"), lax.axis_index("depth")
    blocks, slabs = lax.axis_size("tm"), lax.axis_size("depth")
    left, right = lax.rem(me + blocks - 1, blocks), lax.rem(me + 1, blocks)
    below, above = lax.rem(level + slabs - 1, slabs), lax.rem(level + 1, slabs)
    slow = lax.rem(me, 2)

    load = pltpu.make_async_copy(iq_any, own16, load_sem)
    load.start()
    barrier = pltpu.get_barrier_semaphore()
    for target in ((left, level), (right, level), (me, below), (me, above)):
        pl.semaphore_signal(barrier, inc=1, device_id=target, device_id_type=MESH)
    load.wait()

    def scale_frame(f, carry):
        for c in range(2):
            value = own16[c, f] * jnp.bfloat16(0.5)
            own16[c, f] = value
            wide = value.astype(jnp.float32)
            for s in range(2):
                field[2 * f + s, c, HMAX : HMAX + depth] = wide[:, s * strip : (s + 1) * strip]
        first = [own16[c, f, 0:16].astype(jnp.float32)[:HMAX] for c in range(2)]
        last = [own16[c, f, depth - 16 : depth].astype(jnp.float32)[16 - HMAX :] for c in range(2)]
        edge_out[0, f] = jnp.concatenate(first, axis=0).astype(jnp.bfloat16)
        edge_out[1, f] = jnp.concatenate(last, axis=0).astype(jnp.bfloat16)
        return carry

    lax.fori_loop(0, frames, scale_frame, 0)
    pl.semaphore_wait(barrier, 4)

    def edge_copy(way):
        return pltpu.make_async_remote_copy(
            src_ref=edge_out.at[way],
            dst_ref=edge_in.at[1 - way],
            send_sem=edge_send.at[way],
            recv_sem=edge_recv.at[1 - way],
            device_id=(me, below if way == 0 else above),
            device_id_type=MESH,
        )

    def near_copy(side, j):
        frame = j if side == 0 else frames - 1 - j
        return pltpu.make_async_remote_copy(
            src_ref=own16.at[:, frame, :, pl.ds(side * strip, strip)],
            dst_ref=near16.at[1 - side, j],
            send_sem=near_send.at[side, j],
            recv_sem=near_recv.at[1 - side, j],
            device_id=(left if side == 0 else right, level),
            device_id_type=MESH,
        )

    def far_copy(side):
        return pltpu.make_async_remote_copy(
            src_ref=edge_in.at[:, :, :, pl.ds(side * strip, strip)],
            dst_ref=near_edge.at[1 - side],
            send_sem=far_send.at[side],
            recv_sem=far_recv.at[1 - side],
            device_id=(left if side == 0 else right, level),
            device_id_type=MESH,
        )

    def back_copy(side, j):
        return pltpu.make_async_remote_copy(
            src_ref=total.at[2 * frames + frames * side + j],
            dst_ref=back.at[1 - side, j],
            send_sem=back_send.at[side, j],
            recv_sem=back_recv.at[1 - side, j],
            device_id=(lax.rem(me + blocks - 1 + 2 * side, blocks), level),
            device_id_type=MESH,
        )

    for way in range(2):
        edge_copy(way).start()
    for j in range(frames):
        for side in range(2):
            near_copy(side, j).start()

    column = lax.broadcasted_iota(jnp.int32, (1, 4 * rows), 1)
    place = lax.rem(column, rows) - HMAX
    upper = column < 2 * rows
    for z in range(depth):
        keep = jnp.abs(place - z) <= half[z]
        band[z : z + 1] = jnp.where(keep & upper, 1.0, 0.0)
        band[depth + z : depth + z + 1] = jnp.where(keep & jnp.logical_not(upper), 1.0, 0.0)
    window = band[...].astype(jnp.bfloat16)
    total[...] = jnp.zeros_like(total)
    sums[...] = jnp.zeros_like(sums)

    low_factor = jnp.where(level > 0, 1.0, 0.0)
    high_factor = jnp.where(level < slabs - 1, 1.0, 0.0)

    def put_edges(slot, low, high):
        low = low.astype(jnp.float32) * low_factor
        high = high.astype(jnp.float32) * high_factor
        for c in range(2):
            field[slot, c, 0:HMAX] = low[c * HMAX : (c + 1) * HMAX]
            field[slot, c, HMAX + depth : rows] = high[c * HMAX : (c + 1) * HMAX]

    for way in range(2):
        edge_copy(way).wait_recv()
    for side in range(2):
        far_copy(side).start()

    def own_edges(f, carry):
        for s in range(2):
            cut = pl.ds(s * strip, strip)
            put_edges(2 * f + s, edge_in[0, f, :, cut], edge_in[1, f, :, cut])
        return carry

    lax.fori_loop(0, frames, own_edges, 0)

    left_valid = jnp.where(me > 0, 1.0, 0.0)
    right_valid = jnp.where(me < blocks - 1, 1.0, 0.0)

    def wait_far(side):
        pltpu.make_async_remote_copy(
            src_ref=edge_in.at[:, :, :, pl.ds(0, strip)],
            dst_ref=near_edge.at[side],
            send_sem=far_send.at[side],
            recv_sem=far_recv.at[side],
            device_id=(left, level),
            device_id_type=MESH,
        ).wait_recv()

    def take_near(side, j):
        pltpu.make_async_remote_copy(
            src_ref=own16.at[:, 0, :, pl.ds(0, strip)],
            dst_ref=near16.at[side, j],
            send_sem=near_send.at[side, j],
            recv_sem=near_recv.at[side, j],
            device_id=(left, level),
            device_id_type=MESH,
        ).wait_recv()
        slot = 2 * frames + frames * side + j
        for c in range(2):
            field[slot, c, HMAX : HMAX + depth] = near16[side, j, c].astype(jnp.float32)
        frame = frames - 1 - j + side * (2 * j - frames + 1)
        put_edges(slot, near_edge[side, 0, frame], near_edge[side, 1, frame])

    def unit(n, q):
        inner = 1 - at_least(n, HEAD) + at_least(n, HEAD + EDGE_STEPS)
        nb = n - EDGE_STEPS * at_least(n, HEAD + EDGE_STEPS)
        row = q // 2
        if row == 0:
            first, last = 0, 1 + nb
        elif row == 1:
            fold = at_least(nb, 4)
            first, last = 1 + 3 * fold, 2 + nb - fold
        else:
            fold = at_least(nb, 3)
            first, last = 2 + fold, 3 + nb - 2 * fold
        v = (n - HEAD) * UNITS + q
        second = at_least(v, 21)
        v = v - 21 * second
        side = slow + second * (1 - 2 * slow)
        j = sum(at_least(v, bound) for bound in (6, 11, 15, 18, 20))
        e = v - (6 * j - (j * (j - 1)) // 2)
        mine = 2 * (e + side * (frames - 1 - 2 * e)) + 1 - side
        theirs = 2 * frames + frames * side + j
        early = theirs + side * (mine - theirs)
        late = mine + side * (theirs - mine)
        is_inner = inner > 0
        early = jnp.where(is_inner, 2 * first + q % 2, early)
        late = jnp.where(is_inner, 2 * last + q % 2, late)
        lag = jnp.where(is_inner, last - first, 1 + j + e)
        valid = jnp.where(is_inner, 1.0, jnp.where(side > 0, right_valid, left_valid))
        weight = weights[lag - 1].astype(jnp.float32) * valid
        return early, late, weight

    def windowed(early, late):
        ar, ai = field[early, 0], field[early, 1]
        br, bi = field[late, 0], field[late, 1]
        parts = []
        for value in (br * ar + bi * ai, bi * ar - br * ai):
            high = value.astype(jnp.bfloat16)
            low = (value - high.astype(jnp.float32)).astype(jnp.bfloat16)
            parts += [high, low]
        return jnp.dot(window, jnp.concatenate(parts, axis=0), preferred_element_type=jnp.float32)

    def finish(q, early, late, weight):
        for g in range(0, depth, 24):
            part = pl.ds(g, 24)
            phase = signed_phase(sums[q, pl.ds(depth + g, 24)], sums[q, part], weight)
            total[early, part] = total[early, part] + phase
            total[late, part] = total[late, part] + phase

    def step(n, carry):
        near = n - HEAD

        @pl.when(near == 0)
        def _():
            wait_far(slow)
            take_near(slow, 0)

        @pl.when(near == 1)
        def _():
            take_near(slow, 1)
            take_near(slow, 2)

        @pl.when(near == 2)
        def _():
            take_near(slow, 3)

        @pl.when(near == 3)
        def _():
            take_near(slow, 4)
            take_near(slow, 5)
            wait_far(1 - slow)
            take_near(1 - slow, 0)

        @pl.when(near == 4)
        def _():
            take_near(1 - slow, 1)

        @pl.when(near == 5)
        def _():
            take_near(1 - slow, 2)

        @pl.when(near == 6)
        def _():
            take_near(1 - slow, 3)
            take_near(1 - slow, 4)
            take_near(1 - slow, 5)

        before = jnp.maximum(n - 1, 0)
        started = jnp.where(n > 0, 1.0, 0.0)
        for q in range(UNITS):
            early, late, _ = unit(n, q)
            result = windowed(early, late)
            early, late, weight = unit(before, q)
            finish(q, early, late, weight * started)
            sums[q] = result

        @pl.when(near == 1)
        def _():
            back_copy(slow, 0).start()

        @pl.when(near == 2)
        def _():
            back_copy(slow, 1).start()

        @pl.when(near == 3)
        def _():
            back_copy(slow, 2).start()
            back_copy(slow, 3).start()

        @pl.when(near == 4)
        def _():
            back_copy(slow, 4).start()
            back_copy(slow, 5).start()

        @pl.when(near == 5)
        def _():
            back_copy(1 - slow, 0).start()

        @pl.when(near == 6)
        def _():
            back_copy(1 - slow, 1).start()
            back_copy(1 - slow, 2).start()

        @pl.when(near == 7)
        def _():
            back_copy(1 - slow, 3).start()
            back_copy(1 - slow, 4).start()
            back_copy(1 - slow, 5).start()

        return carry

    lax.fori_loop(0, STEPS, step, 0)
    for q in range(UNITS):
        early, late, weight = unit(jnp.int32(STEPS - 1), q)
        finish(q, early, late, weight)

    for way in range(2):
        edge_copy(way).wait_send()
    for side in range(2):
        far_copy(side).wait_send()
        for j in range(frames):
            near_copy(side, j).wait_send()
            back_copy(side, j).wait()

    frame_total = frames * blocks
    for f in range(frames):
        now = me * frames + f
        norm = jnp.float32(0.0)
        for lag in range(1, LAGS + 1):
            count = jnp.where(now + lag < frame_total, 1.0, 0.0) + jnp.where(now - lag >= 0, 1.0, 0.0)
            norm = norm + weights[lag - 1].astype(jnp.float32) * count
        inverse = 1.0 / jnp.full((8, strip), norm, jnp.float32)
        for g in range(0, depth, 8):
            part = pl.ds(g, 8)
            out[f, part, 0:strip] = (total[2 * f, part] + back[0, f, part]) * inverse
            out[f, part, strip:lines] = (total[2 * f + 1, part] + back[1, frames - 1 - f, part]) * inverse


def shards(iq, half, weights):
    _, frames, depth, lines = iq.shape
    strip = lines // 2
    rows = depth + 2 * HMAX
    slots = 4 * frames
    dma = pltpu.SemaphoreType.DMA
    return pl.pallas_call(
        kernel,
        out_shape=jax.ShapeDtypeStruct((frames, depth, lines), jnp.float32),
        in_specs=[
            pl.BlockSpec(memory_space=pl.ANY),
            pl.BlockSpec(memory_space=pltpu.SMEM),
            pl.BlockSpec(memory_space=pltpu.SMEM),
        ],
        out_specs=pl.BlockSpec(memory_space=pltpu.VMEM),
        scratch_shapes=[
            pltpu.VMEM((2, frames, depth, lines), jnp.bfloat16),
            pltpu.VMEM((2, frames, 2 * HMAX, lines), jnp.bfloat16),
            pltpu.VMEM((2, frames, 2 * HMAX, lines), jnp.bfloat16),
            pltpu.VMEM((2, frames, 2, depth, strip), jnp.bfloat16),
            pltpu.VMEM((2, 2, frames, 2 * HMAX, strip), jnp.bfloat16),
            pltpu.VMEM((slots, 2, rows, strip), jnp.float32),
            pltpu.VMEM((slots, depth, strip), jnp.float32),
            pltpu.VMEM((UNITS, 2 * depth, strip), jnp.float32),
            pltpu.VMEM((2 * depth, 4 * rows), jnp.float32),
            pltpu.VMEM((2, frames, depth, strip), jnp.float32),
            dma(()),
            dma((2,)),
            dma((2,)),
            dma((2, frames)),
            dma((2, frames)),
            dma((2,)),
            dma((2,)),
            dma((2, frames)),
            dma((2, frames)),
        ],
        compiler_params=pltpu.CompilerParams(
            collective_id=0, has_side_effects=True, vmem_limit_bytes=32 * 1024 * 1024
        ),
        name="pair_phases",
    )(iq, half, weights)


def solution(mesh):
    placed = (P(None, "tm", "depth", None), P("depth"), P())
    return jax.shard_map(
        shards, mesh=mesh, in_specs=placed, out_specs=P("tm", "depth", None), check_vma=False
    )
```

time: 93.9 us -> 29.6 us (0.32)
  the two profiles are of different devices: /device:TPU:128 before, /device:TPU:8 now
where the time goes in v1:
time: 29.6 us; the launch traced here: 29.5 us
  Pallas kernels  26.3 us (89%)
  local copies, waits for them, and re-layouts  3.19 us (11%)
    pallas_call x1, Pallas kernels, shards(): pl.pallas_call(kernel, out_shape=jax.ShapeDtypeStruct((frames, depth, lin...  26.3 us
    unnamed x7, local copies, waits for them, and re-layouts  3.19 us

profile of v1, /device:TPU:8, one launch (start us, length us, event | category | flops | bytes accessed | tf_op | source)
XLA Modules:
  0.0 29.5 jit_solution(1324821381481240398)
XLA Ops:
  0.0 0.0 copy-start
  0.0 1.1 %copy-done = bf16[2,6,48,512]{3,2,1,0:T(8,128)(2,1)S(1)} copy-done((bf16[2,6,48,512]{3,2,1,0:T(8,128)(2,1)S(1)}, bf16[2,6,48,512]{3,2,1,0:T(8,128)(2,1)}, u32[]{:S(2)}) %copy-start) | copy-done | bytes 589848
  1.1 0.0 copy-start.1
  1.1 0.7 %copy-done.1 = s32[48]{0:T(128)S(1)} copy-done((s32[48]{0:T(128)S(1)}, s32[48]{0:T(128)}, u32[]{:S(2)}) %copy-start.1) | copy-done | bytes 216
  1.7 0.0 copy-start.2
  1.7 0.7 %copy-done.2 = s32[6]{0:T(128)S(1)} copy-done((s32[6]{0:T(128)S(1)}, s32[6]{0:T(128)}, u32[]{:S(2)}) %copy-start.2) | copy-done | bytes 48
  2.4 26.3 %pair_phases.1 = f32[6,48,512]{2,1,0:T(8,128)S(1)} custom-call(bf16[2,6,48,512]{3,2,1,0:T(8,128)(2,1)S(1)} %copy-done, s32[48]{0:T(128)S(1)} %copy-done.1, s32[6]{0:T(128)S(1)} %copy-done.2), custom_call_target="tpu_custom_call" | custom-call | tf_op jit(solution)/shard_map/pair_phases/pallas_call | solution.py:358
  28.7 0.8 %copy.5 = f32[6,48,512]{2,1,0:T(8,128)} copy(f32[6,48,512]{2,1,0:T(8,128)S(1)} %pair_phases.1) | data formatting | bytes 1179648
Async XLA Ops:
  0.0 1.1 %copy-start = (bf16[2,6,48,512]{3,2,1,0:T(8,128)(2,1)S(1)}, bf16[2,6,48,512]{3,2,1,0:T(8,128)(2,1)}, u32[]{:S(2)}) copy-start(bf16[2,6,48,512]{3,2,1,0:T(8,128)(2,1)} %iq_any.1) | copy-start | bytes 1769476
  1.1 0.7 %copy-start.1 = (s32[48]{0:T(128)S(1)}, s32[48]{0:T(128)}, u32[]{:S(2)}) copy-start(s32[48]{0:T(128)} %half.1) | copy-start | bytes 580
  1.7 0.7 %copy-start.2 = (s32[6]{0:T(128)S(1)}, s32[6]{0:T(128)}, u32[]{:S(2)}) copy-start(s32[6]{0:T(128)} %weights.1) | copy-start | bytes 76

commit v2 on v1

--- a/solution.py
+++ b/solution.py
@@ -24,7 +24,7 @@
 MESH = pl.DeviceIdType.MESH
 UNITS = 6
 STEPS = 12
-HEAD = 4
+HEAD = 1
 EDGE_STEPS = 7
 
 
@@ -48,9 +48,9 @@
 
 
 def kernel(
-    iq_any, half, weights, out,
-    own16, edge_out, edge_in, near16, near_edge, field, total, sums, band, back,
-    load_sem, edge_send, edge_recv, near_send, near_recv, far_send, far_recv, back_send, back_recv,
+    iq_any, half_any, weights_any, out,
+    half, weights, own16, edge_out, edge_in, near16, near_edge, field, total, sums, band, back,
+    load_sem, small_sem, edge_send, edge_recv, near_send, near_recv, far_send, far_recv, back_send, back_recv,
 ):
     frames, depth, lines = own16.shape[1:]
     strip = lines // 2
@@ -63,9 +63,23 @@
 
     load = pltpu.make_async_copy(iq_any, own16, load_sem)
     load.start()
+    small = [
+        pltpu.make_async_copy(half_any, half, small_sem.at[0]),
+        pltpu.make_async_copy(weights_any, weights, small_sem.at[1]),
+    ]
+    for copy in small:
+        copy.start()
+    beside = (me > 0, me < blocks - 1)
     barrier = pltpu.get_barrier_semaphore()
-    for target in ((left, level), (right, level), (me, below), (me, above)):
-        pl.semaphore_signal(barrier, inc=1, device_id=target, device_id_type=MESH)
+    for other in (below, above):
+        pl.semaphore_signal(barrier, inc=1, device_id=(me, other), device_id_type=MESH)
+    for side, column in enumerate((left, right)):
+
+        @pl.when(beside[side])
+        def _(column=column):
+            for other in (level, below, above):
+                pl.semaphore_signal(barrier, inc=1, device_id=(column, other), device_id_type=MESH)
+
     load.wait()
 
     def scale_frame(f, carry):
@@ -82,7 +96,7 @@
         return carry
 
     lax.fori_loop(0, frames, scale_frame, 0)
-    pl.semaphore_wait(barrier, 4)
+    pl.semaphore_wait(barrier, 2 + 3 * sum(side.astype(jnp.int32) for side in beside))
 
     def edge_copy(way):
         return pltpu.make_async_remote_copy(
@@ -105,13 +119,13 @@
             device_id_type=MESH,
         )
 
-    def far_copy(side):
+    def far_copy(side, way):
         return pltpu.make_async_remote_copy(
-            src_ref=edge_in.at[:, :, :, pl.ds(side * strip, strip)],
-            dst_ref=near_edge.at[1 - side],
-            send_sem=far_send.at[side],
-            recv_sem=far_recv.at[1 - side],
-            device_id=(left if side == 0 else right, level),
+            src_ref=edge_out.at[way, :, :, pl.ds(side * strip, strip)],
+            dst_ref=near_edge.at[1 - side, 1 - way],
+            send_sem=far_send.at[side, way],
+            recv_sem=far_recv.at[1 - side, 1 - way],
+            device_id=(left if side == 0 else right, below if way == 0 else above),
             device_id_type=MESH,
         )
 
@@ -127,9 +141,22 @@
 
     for way in range(2):
         edge_copy(way).start()
+    for side in range(2):
+
+        @pl.when(beside[side])
+        def _(side=side):
+            for way in range(2):
+                far_copy(side, way).start()
+
     for j in range(frames):
         for side in range(2):
-            near_copy(side, j).start()
+
+            @pl.when(beside[side])
+            def _(side=side, j=j):
+                near_copy(side, j).start()
+
+    for copy in small:
+        copy.wait()
 
     column = lax.broadcasted_iota(jnp.int32, (1, 4 * rows), 1)
     place = lax.rem(column, rows) - HMAX
@@ -141,6 +168,12 @@
     window = band[...].astype(jnp.bfloat16)
     total[...] = jnp.zeros_like(total)
     sums[...] = jnp.zeros_like(sums)
+    for side in range(2):
+
+        @pl.when(jnp.logical_not(beside[side]))
+        def _(side=side):
+            back[side] = jnp.zeros_like(back[side])
+
 
     low_factor = jnp.where(level > 0, 1.0, 0.0)
     high_factor = jnp.where(level < slabs - 1, 1.0, 0.0)
@@ -154,9 +187,6 @@
 
     for way in range(2):
         edge_copy(way).wait_recv()
-    for side in range(2):
-        far_copy(side).start()
-
     def own_edges(f, carry):
         for s in range(2):
             cut = pl.ds(s * strip, strip)
@@ -168,30 +198,49 @@
     left_valid = jnp.where(me > 0, 1.0, 0.0)
     right_valid = jnp.where(me < blocks - 1, 1.0, 0.0)
 
+    def at_side(side):
+        target = me - 1 + 2 * side
+        return (target >= 0) & (target < blocks)
+
     def wait_far(side):
-        pltpu.make_async_remote_copy(
-            src_ref=edge_in.at[:, :, :, pl.ds(0, strip)],
-            dst_ref=near_edge.at[side],
-            send_sem=far_send.at[side],
-            recv_sem=far_recv.at[side],
-            device_id=(left, level),
-            device_id_type=MESH,
-        ).wait_recv()
+        @pl.when(at_side(side))
+        def _():
+            for way in range(2):
+                pltpu.make_async_remote_copy(
+                    src_ref=edge_out.at[way, :, :, pl.ds(0, strip)],
+                    dst_ref=near_edge.at[side, way],
+                    send_sem=far_send.at[side, way],
+                    recv_sem=far_recv.at[side, way],
+                    device_id=(left, level),
+                    device_id_type=MESH,
+                ).wait_recv()
 
     def take_near(side, j):
-        pltpu.make_async_remote_copy(
-            src_ref=own16.at[:, 0, :, pl.ds(0, strip)],
-            dst_ref=near16.at[side, j],
-            send_sem=near_send.at[side, j],
-            recv_sem=near_recv.at[side, j],
-            device_id=(left, level),
-            device_id_type=MESH,
-        ).wait_recv()
         slot = 2 * frames + frames * side + j
-        for c in range(2):
-            field[slot, c, HMAX : HMAX + depth] = near16[side, j, c].astype(jnp.float32)
-        frame = frames - 1 - j + side * (2 * j - frames + 1)
-        put_edges(slot, near_edge[side, 0, frame], near_edge[side, 1, frame])
+
+        @pl.when(at_side(side))
+        def _():
+            pltpu.make_async_remote_copy(
+                src_ref=own16.at[:, 0, :, pl.ds(0, strip)],
+                dst_ref=near16.at[side, j],
+                send_sem=near_send.at[side, j],
+                recv_sem=near_recv.at[side, j],
+                device_id=(left, level),
+                device_id_type=MESH,
+            ).wait_recv()
+            for c in range(2):
+                field[slot, c, HMAX : HMAX + depth] = near16[side, j, c].astype(jnp.float32)
+            frame = frames - 1 - j + side * (2 * j - frames + 1)
+            put_edges(slot, near_edge[side, 0, frame], near_edge[side, 1, frame])
+
+        @pl.when(jnp.logical_not(at_side(side)))
+        def _():
+            field[slot] = jnp.zeros_like(field[slot])
+
+    def send_back(side, j):
+        @pl.when(at_side(side))
+        def _():
+            back_copy(side, j).start()
 
     def unit(n, q):
         inner = 1 - at_least(n, HEAD) + at_least(n, HEAD + EDGE_STEPS)
@@ -289,36 +338,36 @@
 
         @pl.when(near == 1)
         def _():
-            back_copy(slow, 0).start()
+            send_back(slow, 0)
 
         @pl.when(near == 2)
         def _():
-            back_copy(slow, 1).start()
+            send_back(slow, 1)
 
         @pl.when(near == 3)
         def _():
-            back_copy(slow, 2).start()
-            back_copy(slow, 3).start()
+            send_back(slow, 2)
+            send_back(slow, 3)
 
         @pl.when(near == 4)
         def _():
-            back_copy(slow, 4).start()
-            back_copy(slow, 5).start()
+            send_back(slow, 4)
+            send_back(slow, 5)
 
         @pl.when(near == 5)
         def _():
-            back_copy(1 - slow, 0).start()
+            send_back(1 - slow, 0)
 
         @pl.when(near == 6)
         def _():
-            back_copy(1 - slow, 1).start()
-            back_copy(1 - slow, 2).start()
+            send_back(1 - slow, 1)
+            send_back(1 - slow, 2)
 
         @pl.when(near == 7)
         def _():
-            back_copy(1 - slow, 3).start()
-            back_copy(1 - slow, 4).start()
-            back_copy(1 - slow, 5).start()
+            send_back(1 - slow, 3)
+            send_back(1 - slow, 4)
+            send_back(1 - slow, 5)
 
         return carry
 
@@ -330,10 +379,16 @@
     for way in range(2):
         edge_copy(way).wait_send()
     for side in range(2):
-        far_copy(side).wait_send()
-        for j in range(frames):
-            near_copy(side, j).wait_send()
-            back_copy(side, j).wait()
+
+        @pl.when(beside[side])
+        def _(side=side):
+            for way in range(2):
+                far_copy(side, way).wait_send()
+            for j in range(frames):
+                near_copy(side, j).wait_send()
+                back_copy(side, j).wait_send()
+                back_copy(1 - side, j).wait_recv()
+
 
     frame_total = frames * blocks
     for f in range(frames):
@@ -357,14 +412,16 @@
     dma = pltpu.SemaphoreType.DMA
     return pl.pallas_call(
         kernel,
-        out_shape=jax.ShapeDtypeStruct((frames, depth, lines), jnp.float32),
+        out_shape=pltpu.VMEM((frames, depth, lines), jnp.float32),
         in_specs=[
-            pl.BlockSpec(memory_space=pl.ANY),
-            pl.BlockSpec(memory_space=pltpu.SMEM),
-            pl.BlockSpec(memory_space=pltpu.SMEM),
+            pl.BlockSpec(memory_space=pltpu.HBM),
+            pl.BlockSpec(memory_space=pltpu.HBM),
+            pl.BlockSpec(memory_space=pltpu.HBM),
         ],
         out_specs=pl.BlockSpec(memory_space=pltpu.VMEM),
         scratch_shapes=[
+            pltpu.SMEM(half.shape, jnp.int32),
+            pltpu.SMEM(weights.shape, jnp.int32),
             pltpu.VMEM((2, frames, depth, lines), jnp.bfloat16),
             pltpu.VMEM((2, frames, 2 * HMAX, lines), jnp.bfloat16),
             pltpu.VMEM((2, frames, 2 * HMAX, lines), jnp.bfloat16),
@@ -378,18 +435,19 @@
             dma(()),
             dma((2,)),
             dma((2,)),
+            dma((2,)),
             dma((2, frames)),
             dma((2, frames)),
-            dma((2,)),
-            dma((2,)),
+            dma((2, 2)),
+            dma((2, 2)),
             dma((2, frames)),
             dma((2, frames)),
         ],
         compiler_params=pltpu.CompilerParams(
-            collective_id=0, has_side_effects=True, vmem_limit_bytes=32 * 1024 * 1024
+            collective_id=0, has_side_effects=True, vmem_limit_bytes=48 * 1024 * 1024
         ),
         name="pair_phases",
-    )(iq, half, weights)
+    )(*(pltpu.with_memory_space_constraint(x, pltpu.HBM) for x in (iq, half, weights)))
 
 
 def solution(mesh):

time: 29.6 us -> 21.8 us (0.74)
  the two profiles are of different devices: /device:TPU:8 before, /device:TPU:103 now
where the time goes in v2:
time: 21.8 us; the launch traced here: 21.7 us
  Pallas kernels  20.9 us (96%)
  local copies, waits for them, and re-layouts  0.82 us (4%)
    pallas_call x1, Pallas kernels, shards(): pl.pallas_call(kernel, out_shape=pltpu.VMEM((frames, depth, lines), jnp.f...  20.9 us
    unnamed x1, local copies, waits for them, and re-layouts  0.82 us

profile of v2, /device:TPU:103, one launch (start us, length us, event | category | flops | bytes accessed | tf_op | source)
XLA Modules:
  0.0 21.7 jit_solution(14647974016993870459)
XLA Ops:
  0.0 20.9 %pair_phases.1 = f32[6,48,512]{2,1,0:T(8,128)S(1)} custom-call(bf16[2,6,48,512]{3,2,1,0:T(8,128)(2,1)} %iq_any.1, s32[48]{0:T(128)} %half_any.1, s32[6]{0:T(128)} %weights_any.1), custom_call_target="tpu_custom_call" | custom-call | tf_op jit(solution)/shard_map/pair_phases/pallas_call | solution.py:413
  20.9 0.8 %copy.5 = f32[6,48,512]{2,1,0:T(8,128)} copy(f32[6,48,512]{2,1,0:T(8,128)S(1)} %pair_phases.1) | data formatting | bytes 1179648

commit v3 on v1

v3 whole, which is shorter than its diff:
```python
import functools

import jax
import jax.numpy as jnp
import numpy as np
from jax import lax
from jax.experimental import pallas as pl
from jax.experimental.pallas import tpu as pltpu
from jax.sharding import PartitionSpec as P

LAGS = 6
HMAX = 8
HALF_PI = float(np.float32(np.pi / 2))
PI = float(np.float32(np.pi))
TINY = 1.1754944e-38
ATAN = (
    0.9999960660934448,
    -0.33301785588264465,
    0.19582265615463257,
    -0.12176322191953659,
    0.05807745084166527,
    -0.0137208616361022,
)
MESH = pl.DeviceIdType.MESH
UNITS = 6
INNER = 5
OUTER = 7
STEPS = INNER + OUTER
EDGE = 2 * HMAX
NEAR_GROUPS = ((0, 2), (2, 2), (4, 2))
FAR_GROUPS = ((0, 1), (1, 2), (3, 3))


def at_least(value, bound):
    return (value >= bound).astype(jnp.int32)


def signed_phase(y, x, weight):
    ax = jnp.abs(x)
    ay = jnp.abs(y)
    high = jnp.maximum(jnp.maximum(ax, ay), TINY)
    t = jnp.minimum(ax, ay) * pltpu.reciprocal(high, approx=True)
    s = t * t
    poly = ATAN[-1] * s + ATAN[-2]
    for coefficient in ATAN[-3::-1]:
        poly = poly * s + coefficient
    angle = poly * t
    angle = jnp.where(ay > ax, HALF_PI - angle, angle)
    angle = jnp.where(x < 0, PI - angle, angle)
    return angle * jnp.where(y < 0, -weight, weight)


def split_products(early, late):
    parts = []
    (ar, ai), (br, bi) = early, late
    for value in (br * ar + bi * ai, bi * ar - br * ai):
        high = value.astype(jnp.bfloat16)
        low = (value - high.astype(jnp.float32)).astype(jnp.bfloat16)
        parts += [high, low]
    return parts


def kernel(
    iq_any, half_any, weights_any, out,
    half, weights, scaled, own16, edge_out, edge_in, near16, near_edge, field, edges,
    mid_total, edge_total, mid_sums, edge_sums, held, band, edge_band, mid_back, edge_back,
    load_sem, small_sem, edge_send, edge_recv, near_send, near_recv, far_send, far_recv,
    mid_send, mid_recv, rim_send, rim_recv,
):
    frames, depth, lines = own16.shape[1:]
    strip = lines // 2
    mid = depth - EDGE
    me, level = lax.axis_index("tm"), lax.axis_index("depth")
    blocks, slabs = lax.axis_size("tm"), lax.axis_size("depth")
    left, right = lax.rem(me + blocks - 1, blocks), lax.rem(me + 1, blocks)
    below, above = lax.rem(level + slabs - 1, slabs), lax.rem(level + 1, slabs)
    slow = lax.rem(me, 2)
    quick = 1 - slow
    beside = (me > 0, me < blocks - 1)
    target = me - 1 + 2 * slow
    slow_here = (target >= 0) & (target < blocks)

    load = pltpu.make_async_copy(iq_any, own16, load_sem)
    load.start()
    small = [
        pltpu.make_async_copy(half_any, half, small_sem.at[0]),
        pltpu.make_async_copy(weights_any, weights, small_sem.at[1]),
    ]
    for copy in small:
        copy.start()
    barrier = pltpu.get_barrier_semaphore()
    for other in (below, above):
        pl.semaphore_signal(barrier, inc=1, device_id=(me, other), device_id_type=MESH)
    for side, column in enumerate((left, right)):

        @pl.when(beside[side])
        def _(column=column):
            for other in (level, below, above):
                pl.semaphore_signal(barrier, inc=1, device_id=(column, other), device_id_type=MESH)

    load.wait()

    def scale_frame(f, carry):
        first, last = [], []
        for c in range(2):
            value = own16[c, f] * jnp.bfloat16(0.5)
            own16[c, f] = value
            wide = value.astype(jnp.float32)
            for s in range(2):
                field[2 * f + s, c] = wide[:, s * strip : (s + 1) * strip]
            first.append(wide[:HMAX])
            last.append(wide[depth - HMAX :])
        edge_out[0, f] = jnp.concatenate(first, axis=0).astype(jnp.bfloat16)
        edge_out[1, f] = jnp.concatenate(last, axis=0).astype(jnp.bfloat16)
        return carry

    lax.fori_loop(0, frames, scale_frame, 0)
    pl.semaphore_wait(barrier, 2 + 3 * sum(side.astype(jnp.int32) for side in beside))

    def edge_copy(way):
        return pltpu.make_async_remote_copy(
            src_ref=edge_out.at[way],
            dst_ref=edge_in.at[1 - way],
            send_sem=edge_send.at[way],
            recv_sem=edge_recv.at[1 - way],
            device_id=(me, below if way == 0 else above),
            device_id_type=MESH,
        )

    def near_copy(side, j):
        frame = j if side == 0 else frames - 1 - j
        return pltpu.make_async_remote_copy(
            src_ref=own16.at[:, frame, :, pl.ds(side * strip, strip)],
            dst_ref=near16.at[1 - side, j],
            send_sem=near_send.at[side, j],
            recv_sem=near_recv.at[1 - side, j],
            device_id=(left if side == 0 else right, level),
            device_id_type=MESH,
        )

    def far_copy(side, way):
        return pltpu.make_async_remote_copy(
            src_ref=edge_out.at[way, :, :, pl.ds(side * strip, strip)],
            dst_ref=near_edge.at[1 - side, 1 - way],
            send_sem=far_send.at[side, way],
            recv_sem=far_recv.at[1 - side, 1 - way],
            device_id=(left if side == 0 else right, below if way == 0 else above),
            device_id_type=MESH,
        )

    def back_copy(side, group, groups, source, target, send, recv):
        first, count = groups[group]
        return pltpu.make_async_remote_copy(
            src_ref=source.at[pl.ds(2 * frames + frames * side + first, count)],
            dst_ref=target.at[1 - side, pl.ds(first, count)],
            send_sem=send.at[side, group],
            recv_sem=recv.at[1 - side, group],
            device_id=(lax.rem(me + blocks - 1 + 2 * side, blocks), level),
            device_id_type=MESH,
        )

    middle = (mid_total, mid_back, mid_send, mid_recv)
    rim = (edge_total, edge_back, rim_send, rim_recv)

    def send_quick(group, what):
        back_copy(quick, group, NEAR_GROUPS, *what).start()

    def send_slow(group, what):
        @pl.when(slow_here)
        def _():
            back_copy(slow, group, FAR_GROUPS, *what).start()

    for way in range(2):
        edge_copy(way).start()
    for j in range(frames):
        for side in range(2):

            @pl.when(beside[side])
            def _(side=side, j=j):
                near_copy(side, j).start()

    for side in range(2):

        @pl.when(beside[side])
        def _(side=side):
            for way in range(2):
                far_copy(side, way).start()

    for copy in small:
        copy.wait()
    for lag in range(LAGS):
        value = weights[lag].astype(jnp.float32)
        scaled[lag] = value
        scaled[LAGS + lag] = value * jnp.where(slow_here, 1.0, 0.0)

    column = lax.broadcasted_iota(jnp.int32, (1, 4 * depth), 1)
    place = lax.rem(column, depth)
    upper = column < 2 * depth
    for z in range(depth):
        keep = jnp.abs(place - z) <= half[z]
        band[z : z + 1] = jnp.where(keep & upper, 1.0, 0.0)
        band[depth + z : depth + z + 1] = jnp.where(keep & jnp.logical_not(upper), 1.0, 0.0)
    column = lax.broadcasted_iota(jnp.int32, (1, 12 * EDGE), 1)
    which = column // (2 * EDGE)
    place = lax.rem(column, EDGE)
    low_place = jnp.where(place < HMAX, place - HMAX, 4 * depth)
    high_place = jnp.where(place < HMAX, 4 * depth, place - HMAX + depth)
    for row in range(EDGE):
        z = row if row < HMAX else row + mid
        keep = jnp.abs((low_place if row < HMAX else high_place) - z) <= half[z]
        for block in range(6):
            at = block * EDGE + row
            edge_band[at : at + 1] = jnp.where(keep & (which == block), 1.0, 0.0)
    window = band[...].astype(jnp.bfloat16)
    mid_total[...] = jnp.zeros_like(mid_total)
    edge_total[...] = jnp.zeros_like(edge_total)
    mid_sums[...] = jnp.zeros_like(mid_sums)
    edge_sums[...] = jnp.zeros_like(edge_sums)

    @pl.when(jnp.logical_not(slow_here))
    def _():
        mid_back[slow] = jnp.zeros(mid_back.shape[1:], jnp.float32)
        edge_back[slow] = jnp.zeros(edge_back.shape[1:], jnp.float32)

    low_factor = jnp.where(level > 0, 1.0, 0.0)
    high_factor = jnp.where(level < slabs - 1, 1.0, 0.0)

    def put_edges(slot, low, high):
        low = low.astype(jnp.float32) * low_factor
        high = high.astype(jnp.float32) * high_factor
        for c in range(2):
            edges[slot, c, 0:HMAX] = low[c * HMAX : (c + 1) * HMAX]
            edges[slot, c, HMAX:EDGE] = high[c * HMAX : (c + 1) * HMAX]

    def take_near(side, j):
        pltpu.make_async_remote_copy(
            src_ref=own16.at[:, 0, :, pl.ds(0, strip)],
            dst_ref=near16.at[side, j],
            send_sem=near_send.at[side, j],
            recv_sem=near_recv.at[side, j],
            device_id=(left, level),
            device_id_type=MESH,
        ).wait_recv()
        for c in range(2):
            field[2 * frames + frames * side + j, c] = near16[side, j, c].astype(jnp.float32)

    def take_slow(*js):
        @pl.when(slow_here)
        def _():
            for j in js:
                take_near(slow, j)

        @pl.when(jnp.logical_not(slow_here))
        def _():
            for j in js:
                field[2 * frames + frames * slow + j] = jnp.zeros(field.shape[1:], jnp.float32)

    def take_far(side):
        for way in range(2):
            pltpu.make_async_remote_copy(
                src_ref=edge_out.at[way, :, :, pl.ds(0, strip)],
                dst_ref=near_edge.at[side, way],
                send_sem=far_send.at[side, way],
                recv_sem=far_recv.at[side, way],
                device_id=(left, level),
                device_id_type=MESH,
            ).wait_recv()

        def put(j, carry):
            frame = frames - 1 - j + side * (2 * j - frames + 1)
            slot = 2 * frames + frames * side + j
            put_edges(slot, near_edge[side, 0, frame], near_edge[side, 1, frame])
            return carry

        lax.fori_loop(0, frames, put, 0)

    def unit(n, q):
        inner = n < INNER
        row = q // 2
        if row == 0:
            first, last = 0, 1 + n
        elif row == 1:
            fold = at_least(n, 4)
            first, last = 1 + 3 * fold, 2 + n - fold
        else:
            fold = at_least(n, 3)
            first, last = 2 + fold, 3 + n - 2 * fold
        v = (n - INNER) * UNITS + q
        second = at_least(v, 21)
        v = v - 21 * second
        side = quick + second * (slow - quick)
        j = sum(at_least(v, bound) for bound in (6, 11, 15, 18, 20))
        e = v - (6 * j - (j * (j - 1)) // 2)
        mine = 2 * (e + side * (frames - 1 - 2 * e)) + 1 - side
        theirs = 2 * frames + frames * side + j
        early = theirs + side * (mine - theirs)
        late = mine + side * (theirs - mine)
        early = jnp.where(inner, 2 * first + q % 2, early)
        late = jnp.where(inner, 2 * last + q % 2, late)
        lag = jnp.where(inner, last - first - 1, j + e + LAGS * second)
        return early, late, scaled[lag]

    def finish(total, y, x, place, part, weight):
        phase = signed_phase(y, x, weight)
        early, late = place
        total[early, part] = total[early, part] + phase
        total[late, part] = total[late, part] + phase

    def finish_middle(q, early, late, weight):
        for g in range(0, mid, 16):
            part = pl.ds(g, 16)
            finish(
                mid_total, mid_sums[q, 1, part], mid_sums[q, 0, part], (early, late), part, weight
            )

    def finish_edges(q, at, early, late, weight):
        real = edge_sums[q, 0:EDGE] + held[at, 0]
        imag = edge_sums[q, EDGE : 2 * EDGE] + held[at, 1]
        finish(edge_total, imag, real, (early, late), pl.ds(0, EDGE), weight)

    nothing = tuple((jnp.int32(0), jnp.int32(1), jnp.float32(0)) for _ in range(UNITS))

    def middle_step(n, before):
        b = n - INNER

        @pl.when(b == 0)
        def _():
            take_near(quick, 0)

        @pl.when(b == 1)
        def _():
            take_near(quick, 1)
            take_near(quick, 2)

        @pl.when(b == 2)
        def _():
            take_near(quick, 3)

        @pl.when(b == 3)
        def _():
            take_near(quick, 4)
            take_near(quick, 5)
            take_slow(0)

        @pl.when(b == 4)
        def _():
            take_slow(1)

        @pl.when(b == 5)
        def _():
            take_slow(2)

        @pl.when(b == 6)
        def _():
            take_slow(3, 4, 5)

        now = tuple(unit(n, q) for q in range(UNITS))
        for q in range(UNITS):
            early, late, _ = now[q]
            parts = split_products(
                (field[early, 0], field[early, 1]), (field[late, 0], field[late, 1])
            )
            result = jnp.dot(
                window, jnp.concatenate(parts, axis=0), preferred_element_type=jnp.float32
            )
            finish_middle(q, *before[q])
            for c in range(2):
                value = result[c * depth : (c + 1) * depth]
                mid_sums[q, c] = value[HMAX : depth - HMAX]
                held[n * UNITS + q, c, 0:HMAX] = value[:HMAX]
                held[n * UNITS + q, c, HMAX:EDGE] = value[depth - HMAX :]

        for group in range(3):

            @pl.when(b == 2 + group)
            def _(group=group):
                send_quick(group, middle)

        for group in range(2):

            @pl.when(b == 5 + group)
            def _(group=group):
                send_slow(group, middle)

        return now

    before = lax.fori_loop(0, STEPS, middle_step, nothing)
    for q in range(UNITS):
        finish_middle(q, *before[q])
    send_slow(2, middle)

    for way in range(2):
        edge_copy(way).wait_recv()

    def own_edges(f, carry):
        for s in range(2):
            cut = pl.ds(s * strip, strip)
            put_edges(2 * f + s, edge_in[0, f, :, cut], edge_in[1, f, :, cut])
        return carry

    lax.fori_loop(0, frames, own_edges, 0)
    take_far(quick)
    edge_window = edge_band[...].astype(jnp.bfloat16)

    def edge_step(m, before):
        n = lax.rem(m + INNER, STEPS)
        last = lax.rem(m + INNER + STEPS - 1, STEPS)

        @pl.when(m == 3)
        def _():
            @pl.when(slow_here)
            def _():
                take_far(slow)

            @pl.when(jnp.logical_not(slow_here))
            def _():
                def clear(j, carry):
                    edges[2 * frames + frames * slow + j] = jnp.zeros(edges.shape[1:], jnp.float32)
                    return carry

                lax.fori_loop(0, frames, clear, 0)

        now = tuple(unit(n, q) for q in range(UNITS))
        for start in range(0, UNITS, 3):
            parts = []
            for q in range(start, start + 3):
                early, late, _ = now[q]
                parts += split_products(
                    (edges[early, 0], edges[early, 1]), (edges[late, 0], edges[late, 1])
                )
            result = jnp.dot(
                edge_window, jnp.concatenate(parts, axis=0), preferred_element_type=jnp.float32
            )
            for q in range(start, start + 3):
                finish_edges(q, last * UNITS + q, *before[q])
                edge_sums[q] = result[(q - start) * 2 * EDGE : (q - start + 1) * 2 * EDGE]

        for group in range(3):

            @pl.when(m == 2 + group)
            def _(group=group):
                send_quick(group, rim)

            @pl.when(m == 5 + group)
            def _(group=group):
                send_slow(group, rim)

        return now

    before = lax.fori_loop(0, STEPS, edge_step, nothing)
    for q in range(UNITS):
        finish_edges(q, (INNER - 1) * UNITS + q, *before[q])

    frame_total = frames * blocks

    def write(side):
        cut = pl.ds(pl.multiple_of(side * strip, strip), strip)

        def write_frame(f, carry):
            now = me * frames + f
            norm = jnp.float32(0.0)
            for lag in range(1, LAGS + 1):
                count = at_least(frame_total - 1, now + lag) + at_least(now, lag)
                norm = norm + scaled[lag - 1] * count.astype(jnp.float32)
            inverse = 1.0 / jnp.full((8, strip), norm, jnp.float32)
            j = f + side * (frames - 1 - 2 * f)
            slot = 2 * f + side
            for g in range(0, mid, 8):
                part = pl.ds(g, 8)
                value = mid_total[slot, part] + mid_back[side, j, part]
                out[f, pl.ds(HMAX + g, 8), cut] = value * inverse
            for g, row in ((0, 0), (HMAX, depth - HMAX)):
                part = pl.ds(g, HMAX)
                value = edge_total[slot, part] + edge_back[side, j, part]
                out[f, pl.ds(row, HMAX), cut] = value * inverse
            return carry

        lax.fori_loop(0, frames, write_frame, 0)

    def wait_back(side, groups):
        for what in (middle, rim):
            for group in range(3):
                back_copy(side, group, groups, *what).wait_send()
                back_copy(1 - side, group, groups, *what).wait_recv()

    wait_back(quick, NEAR_GROUPS)
    write(quick)

    @pl.when(slow_here)
    def _():
        wait_back(slow, FAR_GROUPS)

    write(slow)

    for way in range(2):
        edge_copy(way).wait_send()
    for side in range(2):

        @pl.when(beside[side])
        def _(side=side):
            for way in range(2):
                far_copy(side, way).wait_send()
            for j in range(frames):
                near_copy(side, j).wait_send()


def shards(iq, half, weights):
    _, frames, depth, lines = iq.shape
    strip = lines // 2
    mid = depth - EDGE
    slots = 4 * frames
    wide, thin = jnp.float32, jnp.bfloat16
    dma = pltpu.SemaphoreType.DMA
    return pl.pallas_call(
        kernel,
        out_shape=pltpu.VMEM((frames, depth, lines), wide),
        in_specs=[pl.BlockSpec(memory_space=pltpu.HBM)] * 3,
        out_specs=pl.BlockSpec(memory_space=pltpu.VMEM),
        scratch_shapes=[
            pltpu.SMEM(half.shape, jnp.int32),
            pltpu.SMEM(weights.shape, jnp.int32),
            pltpu.SMEM((2 * LAGS,), wide),
            pltpu.VMEM((2, frames, depth, lines), thin),
            pltpu.VMEM((2, frames, EDGE, lines), thin),
            pltpu.VMEM((2, frames, EDGE, lines), thin),
            pltpu.VMEM((2, frames, 2, depth, strip), thin),
            pltpu.VMEM((2, 2, frames, EDGE, strip), thin),
            pltpu.VMEM((slots, 2, depth, strip), wide),
            pltpu.VMEM((slots, 2, EDGE, strip), wide),
            pltpu.VMEM((slots, mid, strip), wide),
            pltpu.VMEM((slots, EDGE, strip), wide),
            pltpu.VMEM((UNITS, 2, mid, strip), wide),
            pltpu.VMEM((UNITS, 2 * EDGE, strip), wide),
            pltpu.VMEM((STEPS * UNITS, 2, EDGE, strip), wide),
            pltpu.VMEM((2 * depth, 4 * depth), wide),
            pltpu.VMEM((6 * EDGE, 12 * EDGE), wide),
            pltpu.VMEM((2, frames, mid, strip), wide),
            pltpu.VMEM((2, frames, EDGE, strip), wide),
            dma(()),
            dma((2,)),
            dma((2,)),
            dma((2,)),
            dma((2, frames)),
            dma((2, frames)),
            dma((2, 2)),
            dma((2, 2)),
            dma((2, 3)),
            dma((2, 3)),
            dma((2, 3)),
            dma((2, 3)),
        ],
        compiler_params=pltpu.CompilerParams(
            collective_id=0, has_side_effects=True, vmem_limit_bytes=48 * 1024 * 1024
        ),
        name="pair_phases",
    )(*(pltpu.with_memory_space_constraint(x, pltpu.HBM) for x in (iq, half, weights)))


def solution(mesh):
    placed = (P(None, "tm", "depth", None), P("depth"), P())
    return jax.shard_map(
        shards, mesh=mesh, in_specs=placed, out_specs=P("tm", "depth", None), check_vma=False
    )
```

time: 29.6 us -> 22.3 us (0.75)
  the two profiles are of different devices: /device:TPU:8 before, /device:TPU:103 now
where the time goes in v3:
time: 22.3 us; the launch traced here: 22.2 us
  Pallas kernels  21.4 us (96%)
  local copies, waits for them, and re-layouts  0.82 us (4%)
    pallas_call x1, Pallas kernels, shards(): pl.pallas_call(kernel, out_shape=pltpu.VMEM((frames, depth, lines), wide)...  21.4 us
    unnamed x1, local copies, waits for them, and re-layouts  0.82 us

profile of v3, /device:TPU:103, one launch (start us, length us, event | category | flops | bytes accessed | tf_op | source)
XLA Modules:
  0.0 22.2 jit_solution(7427255690628714066)
XLA Ops:
  0.0 21.4 %pair_phases.1 = f32[6,48,512]{2,1,0:T(8,128)S(1)} custom-call(bf16[2,6,48,512]{3,2,1,0:T(8,128)(2,1)} %iq_any.1, s32[48]{0:T(128)} %half_any.1, s32[6]{0:T(128)} %weights_any.1), custom_call_target="tpu_custom_call" | custom-call | tf_op jit(solution)/shard_map/pair_phases/pallas_call | solution.py:514
  21.4 0.8 %copy.5 = f32[6,48,512]{2,1,0:T(8,128)} copy(f32[6,48,512]{2,1,0:T(8,128)S(1)} %pair_phases.1) | data formatting | bytes 1179648

commit v4 on v0

v4 whole, which is shorter than its diff:
```python
import functools

import jax
import jax.numpy as jnp
import numpy as np
from jax import lax
from jax.experimental import pallas as pl
from jax.experimental.pallas import tpu as pltpu
from jax.sharding import PartitionSpec as P

LAGS = 6
HMAX = 8
HALF_PI = float(np.float32(np.pi / 2))
PI = float(np.float32(np.pi))
TINY = 1.1754944e-38
ATAN = (
    0.9999960660934448,
    -0.33301785588264465,
    0.19582265615463257,
    -0.12176322191953659,
    0.05807745084166527,
    -0.0137208616361022,
)
MESH = pl.DeviceIdType.MESH
UNITS = 3
STEPS = 7
INNER = 10
QUICK = 7
EDGE = 2 * HMAX
SLOW_GROUPS = ((0, 1), (1, 1), (2, 1), (3, 1), (4, 2))


def at_least(value, bound):
    return (value >= bound).astype(jnp.int32)


def signed_phase(y, x, weight):
    ax = jnp.abs(x)
    ay = jnp.abs(y)
    high = jnp.maximum(jnp.maximum(ax, ay), TINY)
    t = jnp.minimum(ax, ay) * pltpu.reciprocal(high, approx=True)
    s = t * t
    poly = ATAN[-1] * s + ATAN[-2]
    for coefficient in ATAN[-3::-1]:
        poly = poly * s + coefficient
    angle = poly * t
    angle = jnp.where(ay > ax, HALF_PI - angle, angle)
    angle = jnp.where(x < 0, PI - angle, angle)
    return angle * jnp.where(y < 0, -weight, weight)


def split_products(early, late):
    parts = []
    (ar, ai), (br, bi) = early, late
    for value in (br * ar + bi * ai, bi * ar - br * ai):
        high = value.astype(jnp.bfloat16)
        low = (value - high.astype(jnp.float32)).astype(jnp.bfloat16)
        parts += [high, low]
    return parts


def kernel(
    iq_any, half_any, weights_any, out,
    half, weights, scaled, own16, edge_out, edge_in, near16, near_edge, field, edges,
    total, sums, held, band, edge_band, back,
    load_sem, small_sem, edge_send, edge_recv, near_send, near_recv, far_send, far_recv,
    back_send, back_recv,
):
    frames, depth, lines = own16.shape[1:]
    strip = lines // 2
    me, level = lax.axis_index("tm"), lax.axis_index("depth")
    blocks, slabs = lax.axis_size("tm"), lax.axis_size("depth")
    left, right = lax.rem(me + blocks - 1, blocks), lax.rem(me + 1, blocks)
    below, above = lax.rem(level + slabs - 1, slabs), lax.rem(level + 1, slabs)
    slow = lax.rem(me, 2)
    quick = 1 - slow
    beside = (me > 0, me < blocks - 1)
    target = me - 1 + 2 * slow
    slow_here = (target >= 0) & (target < blocks)

    load = pltpu.make_async_copy(iq_any, own16, load_sem)
    load.start()
    small = [
        pltpu.make_async_copy(half_any, half, small_sem.at[0]),
        pltpu.make_async_copy(weights_any, weights, small_sem.at[1]),
    ]
    for copy in small:
        copy.start()
    barrier = pltpu.get_barrier_semaphore()
    for other in (below, above):
        pl.semaphore_signal(barrier, inc=1, device_id=(me, other), device_id_type=MESH)
    for side, column in enumerate((left, right)):

        @pl.when(beside[side])
        def _(column=column):
            for other in (level, below, above):
                pl.semaphore_signal(barrier, inc=1, device_id=(column, other), device_id_type=MESH)

    def cut(side):
        return pl.ds(pl.multiple_of(side * strip, strip), strip)

    def next_to(side):
        return lax.rem(me + blocks - 1 + 2 * side, blocks)

    def frame_at(side, j):
        return j + side * (frames - 1 - 2 * j)

    def edge_copy(way):
        return pltpu.make_async_remote_copy(
            src_ref=edge_out.at[way],
            dst_ref=edge_in.at[1 - way],
            send_sem=edge_send,
            recv_sem=edge_recv,
            device_id=(me, below if way == 0 else above),
            device_id_type=MESH,
        )

    def near_copy(side, j):
        return pltpu.make_async_remote_copy(
            src_ref=own16.at[:, frame_at(side, j), :, cut(side)],
            dst_ref=near16.at[1 - side, j],
            send_sem=near_send.at[side],
            recv_sem=near_recv.at[1 - side, j],
            device_id=(next_to(side), level),
            device_id_type=MESH,
        )

    def far_copy(way):
        return pltpu.make_async_remote_copy(
            src_ref=edge_out.at[way, :, :, cut(slow)],
            dst_ref=near_edge.at[1 - slow, 1 - way],
            send_sem=far_send.at[slow],
            recv_sem=far_recv.at[1 - slow],
            device_id=(next_to(slow), below if way == 0 else above),
            device_id_type=MESH,
        )

    def halo_copy():
        return pltpu.make_async_remote_copy(
            src_ref=edge_in.at[:, :, :, cut(quick)],
            dst_ref=near_edge.at[1 - quick],
            send_sem=far_send.at[quick],
            recv_sem=far_recv.at[1 - quick],
            device_id=(next_to(quick), level),
            device_id_type=MESH,
        )

    def back_copy(side, first, count):
        return pltpu.make_async_remote_copy(
            src_ref=total.at[pl.ds(2 * frames + frames * side + first, count)],
            dst_ref=back.at[1 - side, pl.ds(first, count)],
            send_sem=back_send.at[side],
            recv_sem=back_recv.at[1 - side],
            device_id=(next_to(side), level),
            device_id_type=MESH,
        )

    def waiter(ref, send, recv):
        return pltpu.make_async_remote_copy(
            src_ref=ref, dst_ref=ref, send_sem=send, recv_sem=recv,
            device_id=(me, above), device_id_type=MESH,
        )

    def if_slow(act):
        pl.when(slow_here)(act)

    for copy in small:
        copy.wait()
    for lag in range(LAGS):
        value = weights[lag].astype(jnp.float32)
        scaled[lag] = value
        scaled[LAGS + lag] = value * jnp.where(slow_here, 1.0, 0.0)
    sub = lax.broadcasted_iota(jnp.int32, (8, 4 * (depth + EDGE)), 0)
    column = lax.broadcasted_iota(jnp.int32, (8, 4 * (depth + EDGE)), 1)
    halo = lax.rem(column, EDGE)
    halo = jnp.where(halo < HMAX, halo - HMAX, halo - HMAX + depth)
    inside = column < 4 * depth
    place = jnp.where(inside, lax.rem(column, depth), halo)
    upper = column < jnp.where(inside, 2 * depth, 4 * depth + 2 * EDGE)
    reach = []
    for g in range(0, depth, 8):
        value = jnp.full(sub.shape, half[g], jnp.int32)
        for r in range(1, 8):
            value = jnp.where(sub == r, half[g + r], value)
        reach.append(value)
        keep = jnp.abs(place - (sub + g)) <= value
        band[g : g + 8] = jnp.where(keep & upper, 1.0, 0.0)
        band[depth + g : depth + g + 8] = jnp.where(keep & jnp.logical_not(upper), 1.0, 0.0)
    which = column // (2 * EDGE)
    for block in range(16):
        g = 0 if block % 2 == 0 else depth - 8
        keep = jnp.abs(halo - (sub + g)) <= reach[g // 8]
        edge_band[block * 8 : block * 8 + 8] = jnp.where(keep & (which == block // 2), 1.0, 0.0)
    window = band[...].astype(jnp.bfloat16)

    pl.semaphore_wait(barrier, 2 + 3 * sum(side.astype(jnp.int32) for side in beside))

    load.wait()

    for f in range(frames):
        first, last = [], []
        for c in range(2):
            wide = own16[c, f].astype(jnp.float32)
            first.append(wide[:HMAX])
            last.append(wide[depth - HMAX :])
        edge_out[0, f] = jnp.concatenate(first, axis=0).astype(jnp.bfloat16)
        edge_out[1, f] = jnp.concatenate(last, axis=0).astype(jnp.bfloat16)

    for way in range(2):
        edge_copy(way).start()

    @if_slow
    def _():
        for way in range(2):
            far_copy(way).start()
        for j in range(frames):
            near_copy(slow, j).start()

    for j in range(frames):
        near_copy(quick, j).start()

    def own_field(f, carry):
        for c in range(2):
            wide = own16[c, f].astype(jnp.float32) * 0.5
            for s in range(2):
                field[2 * f + s, c] = wide[:, s * strip : (s + 1) * strip]
        return carry

    lax.fori_loop(0, frames, own_field, 0)
    total[...] = jnp.zeros_like(total)
    sums[...] = jnp.zeros_like(sums)

    @pl.when(jnp.logical_not(slow_here))
    def _():
        back[slow] = jnp.zeros(back.shape[1:], jnp.float32)

    low_factor = jnp.where(level > 0, 0.5, 0.0)
    high_factor = jnp.where(level < slabs - 1, 0.5, 0.0)

    def put_edges(slot, low, high):
        low = low.astype(jnp.float32) * low_factor
        high = high.astype(jnp.float32) * high_factor
        for c in range(2):
            edges[slot, c, 0:HMAX] = low[c * HMAX : (c + 1) * HMAX]
            edges[slot, c, HMAX:EDGE] = high[c * HMAX : (c + 1) * HMAX]

    def take_near(side, j):
        waiter(near16.at[side, j], near_send.at[side], near_recv.at[side, j]).wait_recv()
        for c in range(2):
            wide = near16[side, j, c].astype(jnp.float32) * 0.5
            field[2 * frames + frames * side + j, c] = wide

    def take_far(side):
        waiter(near_edge.at[side], far_send.at[side], far_recv.at[side]).wait_recv()
        for j in range(frames):
            frame = frame_at(1 - side, j)
            slot = 2 * frames + frames * side + j
            put_edges(slot, near_edge[side, 0, frame], near_edge[side, 1, frame])

    def finish(place, part, y, x, weight):
        phase = signed_phase(y, x, weight)
        early, late = place
        total[early, part] = total[early, part] + phase
        total[late, part] = total[late, part] + phase

    def inner_unit(n, q):
        c, s = q // 2, q % 2
        rows = ((0, 1 + c), (1, 2 + c) if c < 4 else (4, 5), (2, 3 + c) if c < 3 else (3, 1 + c))
        first, last = (
            jnp.where(n == 0, rows[0][i], jnp.where(n == 1, rows[1][i], rows[2][i])) for i in range(2)
        )
        return 2 * first + s, 2 * last + s, scaled[last - first - 1]

    def outer_unit(side, v, weight_at):
        j = sum(at_least(v, bound) for bound in (6, 11, 15, 18, 20))
        e = v - (6 * j - (j * (j - 1)) // 2)
        mine = 2 * frame_at(side, e) + 1 - side
        theirs = 2 * frames + frames * side + j
        early = theirs + side * (mine - theirs)
        late = mine + side * (theirs - mine)
        return early, late, scaled[weight_at + j + e]

    def middles(units, base):
        results = []
        for q in range(len(units) + 2):
            if q < len(units):
                early, late, _ = units[q]
                parts = split_products(
                    (field[early, 0], field[early, 1]), (field[late, 0], field[late, 1])
                )
                results.append(
                    jnp.dot(
                        window[:, : 4 * depth],
                        jnp.concatenate(parts, axis=0),
                        preferred_element_type=jnp.float32,
                    )
                )
            if q >= 2:
                early, late, weight = units[q - 2]
                real, imag = results[q - 2][:depth], results[q - 2][depth:]
                for c, value in enumerate((real, imag)):
                    held[base + q - 2, c, 0:HMAX] = value[:HMAX]
                    held[base + q - 2, c, HMAX:EDGE] = value[depth - HMAX :]
                for g in range(HMAX, depth - HMAX, 16):
                    finish(
                        (early, late), pl.ds(g, 16), imag[g : g + 16], real[g : g + 16], weight
                    )

    def rims(units, base):
        results = []
        for start in range(0, len(units), 4):
            group = units[start : start + 4]
            parts = []
            for early, late, _ in group:
                parts += split_products(
                    (edges[early, 0], edges[early, 1]), (edges[late, 0], edges[late, 1])
                )
            rows, columns = 2 * EDGE * len(group), 4 * EDGE * len(group)
            result = jnp.dot(
                edge_window[:rows, :columns],
                jnp.concatenate(parts, axis=0),
                preferred_element_type=jnp.float32,
            )
            results += [result[2 * EDGE * k : 2 * EDGE * (k + 1)] for k in range(len(group))]
        for q, (early, late, weight) in enumerate(units):
            real = results[q][:EDGE] + held[base + q, 0]
            imag = results[q][EDGE:] + held[base + q, 1]
            finish((early, late), pl.ds(0, HMAX), imag[:HMAX], real[:HMAX], weight)
            finish((early, late), pl.ds(depth - HMAX, HMAX), imag[HMAX:], real[HMAX:], weight)

    def inner_middles(n, carry):
        middles([inner_unit(n, q) for q in range(INNER)], n * INNER)
        return carry

    def inner_rims(n, carry):
        rims([inner_unit(n, q) for q in range(INNER)], n * INNER)
        return carry

    def quick_middles(n, carry):
        for at, js in ((0, (0, 1)), (1, (2,)), (2, (3, 4, 5))):

            @pl.when(n == at)
            def _(js=js):
                for j in js:
                    take_near(quick, j)

        middles([outer_unit(quick, n * QUICK + q, 0) for q in range(QUICK)], 3 * INNER + n * QUICK)
        return carry

    def quick_rims(n, carry):
        rims([outer_unit(quick, n * QUICK + q, 0) for q in range(QUICK)], 3 * INNER + n * QUICK)
        return carry

    def slow_unit(n, q):
        return outer_unit(slow, n * UNITS + q, LAGS)

    def finish_slow(q, early, late, weight):
        for g in range(0, depth, 24):
            part = pl.ds(g, 24)
            finish((early, late), part, sums[q, pl.ds(depth + g, 24)], sums[q, part], weight)

    def slow_step(n, carry):
        before, now = carry
        for at, js in ((0, (0,)), (2, (1,)), (3, (2,)), (5, (3,)), (6, (4, 5))):

            @pl.when((n == at) & slow_here)
            def _(js=js):
                for j in js:
                    take_near(slow, j)

        after = tuple(slow_unit(jnp.minimum(n + 1, STEPS - 1), q) for q in range(UNITS))
        for q in range(UNITS):
            early, late, _ = now[q]
            parts = split_products(
                (field[early, 0], field[early, 1]), (field[late, 0], field[late, 1])
            ) + split_products(
                (edges[early, 0], edges[early, 1]), (edges[late, 0], edges[late, 1])
            )
            result = jnp.dot(
                window, jnp.concatenate(parts, axis=0), preferred_element_type=jnp.float32
            )
            finish_slow(q, *before[q])
            sums[q] = result

        for at, group in zip((2, 4, 5, 6), SLOW_GROUPS):

            @pl.when((n == at) & slow_here)
            def _(group=group):
                back_copy(slow, *group).start()

        return now, after

    @pl.when(jnp.logical_not(slow_here))
    def _():
        def clear(j, carry):
            slot = 2 * frames + frames * slow + j
            field[slot] = jnp.zeros(field.shape[1:], jnp.float32)
            edges[slot] = jnp.zeros(edges.shape[1:], jnp.float32)
            return carry

        lax.fori_loop(0, frames, clear, 0)

    lax.fori_loop(0, 3, inner_middles, 0)
    lax.fori_loop(0, 3, quick_middles, 0)

    waiter(edge_in, edge_send, edge_recv).wait_recv()
    halo_copy().start()
    for f in range(frames):
        for s in range(2):
            lanes = pl.ds(s * strip, strip)
            put_edges(2 * f + s, edge_in[0, f, :, lanes], edge_in[1, f, :, lanes])

    @if_slow
    def _():
        take_far(slow)

    nothing = tuple((jnp.int32(0), jnp.int32(1), jnp.float32(0)) for _ in range(UNITS))
    start = tuple(slow_unit(jnp.int32(0), q) for q in range(UNITS))
    before, _ = lax.fori_loop(0, STEPS, slow_step, (nothing, start))
    for q in range(UNITS):
        finish_slow(q, *before[q])

    @if_slow
    def _():
        back_copy(slow, *SLOW_GROUPS[-1]).start()

    take_far(quick)
    edge_window = edge_band[...].astype(jnp.bfloat16)
    lax.fori_loop(0, 3, quick_rims, 0)
    back_copy(quick, 0, frames).start()
    lax.fori_loop(0, 3, inner_rims, 0)

    frame_total = frames * blocks

    def write(side):
        lanes = cut(side)

        def write_frame(f, carry):
            now = me * frames + f
            norm = jnp.float32(0.0)
            for lag in range(1, LAGS + 1):
                count = at_least(frame_total - 1, now + lag) + at_least(now, lag)
                norm = norm + scaled[lag - 1] * count.astype(jnp.float32)
            inverse = 1.0 / jnp.full((8, strip), norm, jnp.float32)
            j = frame_at(side, f)
            slot = 2 * f + side
            for g in range(0, depth, 8):
                part = pl.ds(g, 8)
                out[f, part, lanes] = (total[slot, part] + back[side, j, part]) * inverse
            return carry

        lax.fori_loop(0, frames, write_frame, 0)

    def wait_back(side):
        waiter(back.at[side], back_send.at[side], back_recv.at[side]).wait()

    wait_back(quick)
    write(quick)

    @if_slow
    def _():
        wait_back(slow)

    write(slow)

    waiter(edge_out, edge_send, edge_recv).wait_send()
    for side, here in ((quick, True), (slow, slow_here)):

        @pl.when(here)
        def _(side=side):
            waiter(near_edge.at[side], far_send.at[side], far_recv.at[side]).wait_send()
            waiter(near16.at[side], near_send.at[side], near_send.at[side]).wait_send()


def shards(iq, half, weights):
    _, frames, depth, lines = iq.shape
    strip = lines // 2
    slots = 4 * frames
    wide, thin = jnp.float32, jnp.bfloat16
    dma = pltpu.SemaphoreType.DMA
    return pl.pallas_call(
        kernel,
        out_shape=pltpu.VMEM((frames, depth, lines), wide),
        in_specs=[pl.BlockSpec(memory_space=pltpu.HBM)] * 3,
        out_specs=pl.BlockSpec(memory_space=pltpu.VMEM),
        scratch_shapes=[
            pltpu.SMEM(half.shape, jnp.int32),
            pltpu.SMEM(weights.shape, jnp.int32),
            pltpu.SMEM((2 * LAGS,), wide),
            pltpu.VMEM((2, frames, depth, lines), thin),
            pltpu.VMEM((2, frames, EDGE, lines), thin),
            pltpu.VMEM((2, frames, EDGE, lines), thin),
            pltpu.VMEM((2, frames, 2, depth, strip), thin),
            pltpu.VMEM((2, 2, frames, EDGE, strip), thin),
            pltpu.VMEM((slots, 2, depth, strip), wide),
            pltpu.VMEM((slots, 2, EDGE, strip), wide),
            pltpu.VMEM((slots, depth, strip), wide),
            pltpu.VMEM((UNITS, 2 * depth, strip), wide),
            pltpu.VMEM((3 * (INNER + QUICK), 2, EDGE, strip), wide),
            pltpu.VMEM((2 * depth, 4 * (depth + EDGE)), wide),
            pltpu.VMEM((8 * EDGE, 16 * EDGE), wide),
            pltpu.VMEM((2, frames, depth, strip), wide),
            dma(()),
            dma((2,)),
            dma(()),
            dma(()),
            dma((2,)),
            dma((2, frames)),
            dma((2,)),
            dma((2,)),
            dma((2,)),
            dma((2,)),
        ],
        compiler_params=pltpu.CompilerParams(
            collective_id=0, has_side_effects=True, vmem_limit_bytes=48 * 1024 * 1024
        ),
        name="pair_phases",
    )(*(pltpu.with_memory_space_constraint(x, pltpu.HBM) for x in (iq, half, weights)))


def solution(mesh):
    placed = (P(None, "tm", "depth", None), P("depth"), P())
    return jax.shard_map(
        shards, mesh=mesh, in_specs=placed, out_specs=P("tm", "depth", None), check_vma=False
    )
```

time: 93.9 us -> 20.8 us (0.22)
  the two profiles are of different devices: /device:TPU:128 before, /device:TPU:103 now
where the time goes in v4:
time: 20.8 us; the launch traced here: 20.7 us
  Pallas kernels  19.9 us (96%)
  local copies, waits for them, and re-layouts  0.82 us (4%)
    pallas_call x1, Pallas kernels, shards(): pl.pallas_call(kernel, out_shape=pltpu.VMEM((frames, depth, lines), wide)...  19.9 us
    unnamed x1, local copies, waits for them, and re-layouts  0.82 us

profile of v4, /device:TPU:103, one launch (start us, length us, event | category | flops | bytes accessed | tf_op | source)
XLA Modules:
  0.0 20.7 jit_solution(4545314059236203518)
XLA Ops:
  0.0 19.9 %pair_phases.1 = f32[6,48,512]{2,1,0:T(8,128)S(1)} custom-call(bf16[2,6,48,512]{3,2,1,0:T(8,128)(2,1)} %iq_any.1, s32[48]{0:T(128)} %half_any.1, s32[6]{0:T(128)} %weights_any.1), custom_call_target="tpu_custom_call" | custom-call | tf_op jit(solution)/shard_map/pair_phases/pallas_call | solution.py:481
  19.9 0.8 %copy.5 = f32[6,48,512]{2,1,0:T(8,128)} copy(f32[6,48,512]{2,1,0:T(8,128)S(1)} %pair_phases.1) | data formatting | bytes 1179648

commit v5 on v4

--- a/solution.py
+++ b/solution.py
@@ -23,11 +23,10 @@
 )
 MESH = pl.DeviceIdType.MESH
 UNITS = 3
-STEPS = 7
 INNER = 10
 QUICK = 7
 EDGE = 2 * HMAX
-SLOW_GROUPS = ((0, 1), (1, 1), (2, 1), (3, 1), (4, 2))
+SHARED = 3
 
 
 def at_least(value, bound):
@@ -61,10 +60,10 @@
 
 def kernel(
     iq_any, half_any, weights_any, out,
-    half, weights, scaled, own16, edge_out, edge_in, near16, near_edge, field, edges,
-    total, sums, held, band, edge_band, back,
+    half, weights, scaled, own16, edge_out, edge_in, near16, near_edge, more16, more_edge,
+    field, edges, total, held, band, edge_band, back,
     load_sem, small_sem, edge_send, edge_recv, near_send, near_recv, far_send, far_recv,
-    back_send, back_recv,
+    more_send, more_recv, rest_send, rest_recv, back_send, back_recv,
 ):
     frames, depth, lines = own16.shape[1:]
     strip = lines // 2
@@ -135,6 +134,26 @@
             device_id_type=MESH,
         )
 
+    def more_copy(j):
+        return pltpu.make_async_remote_copy(
+            src_ref=own16.at[:, frame_at(slow, j), :, cut(quick)],
+            dst_ref=more16.at[j],
+            send_sem=more_send,
+            recv_sem=more_recv.at[j],
+            device_id=(next_to(slow), level),
+            device_id_type=MESH,
+        )
+
+    def rest_copy(way):
+        return pltpu.make_async_remote_copy(
+            src_ref=edge_out.at[way, pl.ds(slow * (frames - SHARED), SHARED), :, cut(quick)],
+            dst_ref=more_edge.at[1 - way],
+            send_sem=rest_send,
+            recv_sem=rest_recv,
+            device_id=(next_to(slow), below if way == 0 else above),
+            device_id_type=MESH,
+        )
+
     def halo_copy():
         return pltpu.make_async_remote_copy(
             src_ref=edge_in.at[:, :, :, cut(quick)],
@@ -163,6 +182,41 @@
 
     def if_slow(act):
         pl.when(slow_here)(act)
+
+    load.wait()
+
+    for f in range(frames):
+        first, last = [], []
+        for c in range(2):
+            wide = own16[c, f].astype(jnp.float32)
+            first.append(wide[:HMAX])
+            last.append(wide[depth - HMAX :])
+        edge_out[0, f] = jnp.concatenate(first, axis=0).astype(jnp.bfloat16)
+        edge_out[1, f] = jnp.concatenate(last, axis=0).astype(jnp.bfloat16)
+
+    pl.semaphore_wait(barrier, 2 + 3 * sum(side.astype(jnp.int32) for side in beside))
+
+    @if_slow
+    def _():
+        for way in range(2):
+            far_copy(way).start()
+        for j in range(2):
+            near_copy(slow, j).start()
+
+    for way in range(2):
+        edge_copy(way).start()
+
+    @if_slow
+    def _():
+        for j in range(2, frames):
+            near_copy(slow, j).start()
+        for way in range(2):
+            rest_copy(way).start()
+        for j in range(SHARED):
+            more_copy(j).start()
+
+    for j in range(frames):
+        near_copy(quick, j).start()
 
     for copy in small:
         copy.wait()
@@ -193,32 +247,6 @@
         edge_band[block * 8 : block * 8 + 8] = jnp.where(keep & (which == block // 2), 1.0, 0.0)
     window = band[...].astype(jnp.bfloat16)
 
-    pl.semaphore_wait(barrier, 2 + 3 * sum(side.astype(jnp.int32) for side in beside))
-
-    load.wait()
-
-    for f in range(frames):
-        first, last = [], []
-        for c in range(2):
-            wide = own16[c, f].astype(jnp.float32)
-            first.append(wide[:HMAX])
-            last.append(wide[depth - HMAX :])
-        edge_out[0, f] = jnp.concatenate(first, axis=0).astype(jnp.bfloat16)
-        edge_out[1, f] = jnp.concatenate(last, axis=0).astype(jnp.bfloat16)
-
-    for way in range(2):
-        edge_copy(way).start()
-
-    @if_slow
-    def _():
-        for way in range(2):
-            far_copy(way).start()
-        for j in range(frames):
-            near_copy(slow, j).start()
-
-    for j in range(frames):
-        near_copy(quick, j).start()
-
     def own_field(f, carry):
         for c in range(2):
             wide = own16[c, f].astype(jnp.float32) * 0.5
@@ -228,11 +256,11 @@
 
     lax.fori_loop(0, frames, own_field, 0)
     total[...] = jnp.zeros_like(total)
-    sums[...] = jnp.zeros_like(sums)
+    back[slow, SHARED:] = jnp.zeros((frames - SHARED,) + back.shape[2:], jnp.float32)
 
     @pl.when(jnp.logical_not(slow_here))
     def _():
-        back[slow] = jnp.zeros(back.shape[1:], jnp.float32)
+        back[slow, :SHARED] = jnp.zeros((SHARED,) + back.shape[2:], jnp.float32)
 
     low_factor = jnp.where(level > 0, 0.5, 0.0)
     high_factor = jnp.where(level < slabs - 1, 0.5, 0.0)
@@ -256,6 +284,17 @@
             frame = frame_at(1 - side, j)
             slot = 2 * frames + frames * side + j
             put_edges(slot, near_edge[side, 0, frame], near_edge[side, 1, frame])
+
+    def take_more(j):
+        waiter(more16.at[j], more_send, more_recv.at[j]).wait_recv()
+        for c in range(2):
+            field[4 * frames + j, c] = more16[j, c].astype(jnp.float32) * 0.5
+
+    def take_rest():
+        waiter(more_edge, rest_send, rest_recv).wait_recv()
+        for j in range(SHARED):
+            k = SHARED - 1 - j + slow * (2 * j - SHARED + 1)
+            put_edges(4 * frames + j, more_edge[0, k], more_edge[1, k])
 
     def finish(place, part, y, x, weight):
         phase = signed_phase(y, x, weight)
@@ -351,44 +390,74 @@
         rims([outer_unit(quick, n * QUICK + q, 0) for q in range(QUICK)], 3 * INNER + n * QUICK)
         return carry
 
-    def slow_unit(n, q):
-        return outer_unit(slow, n * UNITS + q, LAGS)
-
-    def finish_slow(q, early, late, weight):
-        for g in range(0, depth, 24):
-            part = pl.ds(g, 24)
-            finish((early, late), part, sums[q, pl.ds(depth + g, 24)], sums[q, part], weight)
-
-    def slow_step(n, carry):
-        before, now = carry
-        for at, js in ((0, (0,)), (2, (1,)), (3, (2,)), (5, (3,)), (6, (4, 5))):
-
-            @pl.when((n == at) & slow_here)
-            def _(js=js):
-                for j in js:
-                    take_near(slow, j)
-
-        after = tuple(slow_unit(jnp.minimum(n + 1, STEPS - 1), q) for q in range(UNITS))
-        for q in range(UNITS):
-            early, late, _ = now[q]
-            parts = split_products(
-                (field[early, 0], field[early, 1]), (field[late, 0], field[late, 1])
-            ) + split_products(
-                (edges[early, 0], edges[early, 1]), (edges[late, 0], edges[late, 1])
-            )
-            result = jnp.dot(
-                window, jnp.concatenate(parts, axis=0), preferred_element_type=jnp.float32
-            )
-            finish_slow(q, *before[q])
-            sums[q] = result
-
-        for at, group in zip((2, 4, 5, 6), SLOW_GROUPS):
-
-            @pl.when((n == at) & slow_here)
-            def _(group=group):
-                back_copy(slow, *group).start()
-
-        return now, after
+    def slow_unit(j, e):
+        mine = 2 * frame_at(slow, e) + 1 - slow
+        theirs = 2 * frames + frames * slow + j
+        early = theirs + slow * (mine - theirs)
+        late = mine + slow * (theirs - mine)
+        return early, late, scaled[LAGS + j + e]
+
+    def last_unit(n, q):
+        def pick(values):
+            value = values[3]
+            for k in (2, 1, 0):
+                value = jnp.where(n == k, values[k], value)
+            return value
+
+        j = pick(((3, 4, 0, 1), (3, 4, 0, 1), (3, 5, 0, 2))[q])
+        e = pick(((0, 0, 3, 3), (1, 1, 4, 4), (2, 0, 5, 3))[q])
+        own = jnp.where(n < 2, 1 - slow, slow)
+        mine = 2 * frame_at(slow, e) + own
+        theirs = j + jnp.where(n < 2, 2 * frames + frames * slow, 4 * frames)
+        early = theirs + slow * (mine - theirs)
+        late = mine + slow * (theirs - mine)
+        return early, late, scaled[LAGS + j + e]
+
+    def wholes(units):
+        results = []
+        for q in range(len(units) + 2):
+            if q < len(units):
+                early, late, _ = units[q]
+                parts = split_products(
+                    (field[early, 0], field[early, 1]), (field[late, 0], field[late, 1])
+                ) + split_products(
+                    (edges[early, 0], edges[early, 1]), (edges[late, 0], edges[late, 1])
+                )
+                results.append(
+                    jnp.dot(
+                        window, jnp.concatenate(parts, axis=0), preferred_element_type=jnp.float32
+                    )
+                )
+            if q >= 2:
+                early, late, weight = units[q - 2]
+                real, imag = results[q - 2][:depth], results[q - 2][depth:]
+                for g in range(0, depth, 24):
+                    finish(
+                        (early, late), pl.ds(g, 24), imag[g : g + 24], real[g : g + 24], weight
+                    )
+
+    def last_step(n, carry):
+        @pl.when((n == 0) & slow_here)
+        def _():
+            take_near(slow, 3)
+
+        @pl.when((n == 1) & slow_here)
+        def _():
+            take_near(slow, 4)
+            take_near(slow, 5)
+
+        @pl.when((n == 2) & slow_here)
+        def _():
+            take_rest()
+            take_more(0)
+
+        @pl.when((n == 3) & slow_here)
+        def _():
+            take_more(1)
+            take_more(2)
+
+        wholes([last_unit(n, q) for q in range(UNITS)])
+        return carry
 
     @pl.when(jnp.logical_not(slow_here))
     def _():
@@ -399,6 +468,9 @@
             return carry
 
         lax.fori_loop(0, frames, clear, 0)
+        for j in range(SHARED):
+            field[4 * frames + j] = jnp.zeros(field.shape[1:], jnp.float32)
+            edges[4 * frames + j] = jnp.zeros(edges.shape[1:], jnp.float32)
 
     lax.fori_loop(0, 3, inner_middles, 0)
     lax.fori_loop(0, 3, quick_middles, 0)
@@ -410,25 +482,28 @@
             lanes = pl.ds(s * strip, strip)
             put_edges(2 * f + s, edge_in[0, f, :, lanes], edge_in[1, f, :, lanes])
 
-    @if_slow
-    def _():
-        take_far(slow)
-
-    nothing = tuple((jnp.int32(0), jnp.int32(1), jnp.float32(0)) for _ in range(UNITS))
-    start = tuple(slow_unit(jnp.int32(0), q) for q in range(UNITS))
-    before, _ = lax.fori_loop(0, STEPS, slow_step, (nothing, start))
-    for q in range(UNITS):
-        finish_slow(q, *before[q])
-
-    @if_slow
-    def _():
-        back_copy(slow, *SLOW_GROUPS[-1]).start()
-
+    edge_window = edge_band[...].astype(jnp.bfloat16)
+    lax.fori_loop(0, 3, inner_rims, 0)
+
+    for j in range(SHARED):
+
+        @if_slow
+        def _(j=j):
+            if j == 0:
+                take_far(slow)
+            take_near(slow, j)
+
+        wholes([slow_unit(j, e) for e in range(frames - j)])
+
+        @if_slow
+        def _(j=j):
+            back_copy(slow, j, 1).start()
+
+    lax.fori_loop(0, 2, last_step, 0)
     take_far(quick)
-    edge_window = edge_band[...].astype(jnp.bfloat16)
     lax.fori_loop(0, 3, quick_rims, 0)
     back_copy(quick, 0, frames).start()
-    lax.fori_loop(0, 3, inner_rims, 0)
+    lax.fori_loop(2, 4, last_step, 0)
 
     frame_total = frames * blocks
 
@@ -451,17 +526,19 @@
 
         lax.fori_loop(0, frames, write_frame, 0)
 
-    def wait_back(side):
-        waiter(back.at[side], back_send.at[side], back_recv.at[side]).wait()
-
-    wait_back(quick)
+    waiter(back.at[quick], back_send.at[quick], back_recv.at[quick]).wait()
     write(quick)
 
     @if_slow
     def _():
-        wait_back(slow)
+        waiter(back.at[slow, pl.ds(0, SHARED)], back_send.at[slow], back_recv.at[slow]).wait()
 
     write(slow)
+
+    @if_slow
+    def _():
+        waiter(more_edge, rest_send, rest_recv).wait_send()
+        waiter(more16, more_send, more_send).wait_send()
 
     waiter(edge_out, edge_send, edge_recv).wait_send()
     for side, here in ((quick, True), (slow, slow_here)):
@@ -475,7 +552,7 @@
 def shards(iq, half, weights):
     _, frames, depth, lines = iq.shape
     strip = lines // 2
-    slots = 4 * frames
+    slots = 4 * frames + SHARED
     wide, thin = jnp.float32, jnp.bfloat16
     dma = pltpu.SemaphoreType.DMA
     return pl.pallas_call(
@@ -492,10 +569,11 @@
             pltpu.VMEM((2, frames, EDGE, lines), thin),
             pltpu.VMEM((2, frames, 2, depth, strip), thin),
             pltpu.VMEM((2, 2, frames, EDGE, strip), thin),
+            pltpu.VMEM((SHARED, 2, depth, strip), thin),
+            pltpu.VMEM((2, SHARED, EDGE, strip), thin),
             pltpu.VMEM((slots, 2, depth, strip), wide),
             pltpu.VMEM((slots, 2, EDGE, strip), wide),
             pltpu.VMEM((slots, depth, strip), wide),
-            pltpu.VMEM((UNITS, 2 * depth, strip), wide),
             pltpu.VMEM((3 * (INNER + QUICK), 2, EDGE, strip), wide),
             pltpu.VMEM((2 * depth, 4 * (depth + EDGE)), wide),
             pltpu.VMEM((8 * EDGE, 16 * EDGE), wide),
@@ -508,6 +586,10 @@
             dma((2, frames)),
             dma((2,)),
             dma((2,)),
+            dma(()),
+            dma((SHARED,)),
+            dma(()),
+            dma(()),
             dma((2,)),
             dma((2,)),
         ],

time: 20.8 us -> 18.4 us (0.88)
  Pallas kernels: 19.9 us -> 17.5 us
    pallas_call x1, Pallas kernels: 19.9 us -> 17.5 us  [shards(): pl.pallas_call(kernel, out_shape=pltpu.VMEM((frames, depth, lines), wide)...]
where the time goes in v5:
time: 18.4 us; the launch traced here: 18.3 us
  Pallas kernels  17.5 us (95%)
  local copies, waits for them, and re-layouts  0.82 us (4%)
    pallas_call x1, Pallas kernels, shards(): pl.pallas_call(kernel, out_shape=pltpu.VMEM((frames, depth, lines), wide)...  17.5 us
    unnamed x1, local copies, waits for them, and re-layouts  0.82 us

profile of v5, /device:TPU:103, one launch (start us, length us, event | category | flops | bytes accessed | tf_op | source)
XLA Modules:
  0.0 18.3 jit_solution(4847641226695227981)
XLA Ops:
  0.0 17.5 %pair_phases.1 = f32[6,48,512]{2,1,0:T(8,128)S(1)} custom-call(bf16[2,6,48,512]{3,2,1,0:T(8,128)(2,1)} %iq_any.1, s32[48]{0:T(128)} %half_any.1, s32[6]{0:T(128)} %weights_any.1), custom_call_target="tpu_custom_call" | custom-call | tf_op jit(solution)/shard_map/pair_phases/pallas_call | solution.py:558
  17.5 0.8 %copy.5 = f32[6,48,512]{2,1,0:T(8,128)} copy(f32[6,48,512]{2,1,0:T(8,128)S(1)} %pair_phases.1) | data formatting | bytes 1179648

commit v6 on v5

--- a/solution.py
+++ b/solution.py
@@ -27,6 +27,7 @@
 QUICK = 7
 EDGE = 2 * HMAX
 SHARED = 3
+SHARED_STRIPS = 15
 
 
 def at_least(value, bound):
@@ -116,7 +117,7 @@
 
     def near_copy(side, j):
         return pltpu.make_async_remote_copy(
-            src_ref=own16.at[:, frame_at(side, j), :, cut(side)],
+            src_ref=iq_any.at[:, frame_at(side, j), :, cut(side)],
             dst_ref=near16.at[1 - side, j],
             send_sem=near_send.at[side],
             recv_sem=near_recv.at[1 - side, j],
@@ -164,10 +165,11 @@
             device_id_type=MESH,
         )
 
-    def back_copy(side, first, count):
-        return pltpu.make_async_remote_copy(
-            src_ref=total.at[pl.ds(2 * frames + frames * side + first, count)],
-            dst_ref=back.at[1 - side, pl.ds(first, count)],
+    def back_copy(side, count, part):
+        first = 2 * frames + frames * side
+        return pltpu.make_async_remote_copy(
+            src_ref=total.at[pl.ds(first, count), part],
+            dst_ref=back.at[1 - side, pl.ds(0, count), part],
             send_sem=back_send.at[side],
             recv_sem=back_recv.at[1 - side],
             device_id=(next_to(side), level),
@@ -182,6 +184,14 @@
 
     def if_slow(act):
         pl.when(slow_here)(act)
+
+    total[...] = jnp.zeros_like(total)
+    pl.semaphore_wait(barrier, 2 + 3 * sum(side.astype(jnp.int32) for side in beside))
+
+    @if_slow
+    def _():
+        for j in range(SHARED):
+            near_copy(slow, j).start()
 
     load.wait()
 
@@ -194,21 +204,18 @@
         edge_out[0, f] = jnp.concatenate(first, axis=0).astype(jnp.bfloat16)
         edge_out[1, f] = jnp.concatenate(last, axis=0).astype(jnp.bfloat16)
 
-    pl.semaphore_wait(barrier, 2 + 3 * sum(side.astype(jnp.int32) for side in beside))
 
     @if_slow
     def _():
         for way in range(2):
             far_copy(way).start()
-        for j in range(2):
-            near_copy(slow, j).start()
 
     for way in range(2):
         edge_copy(way).start()
 
     @if_slow
     def _():
-        for j in range(2, frames):
+        for j in range(SHARED, frames):
             near_copy(slow, j).start()
         for way in range(2):
             rest_copy(way).start()
@@ -255,7 +262,6 @@
         return carry
 
     lax.fori_loop(0, frames, own_field, 0)
-    total[...] = jnp.zeros_like(total)
     back[slow, SHARED:] = jnp.zeros((frames - SHARED,) + back.shape[2:], jnp.float32)
 
     @pl.when(jnp.logical_not(slow_here))
@@ -299,8 +305,9 @@
     def finish(place, part, y, x, weight):
         phase = signed_phase(y, x, weight)
         early, late = place
-        total[early, part] = total[early, part] + phase
-        total[late, part] = total[late, part] + phase
+        first, second = total[early, part] + phase, total[late, part] + phase
+        total[early, part] = first
+        total[late, part] = second
 
     def inner_unit(n, q):
         c, s = q // 2, q % 2
@@ -475,6 +482,20 @@
     lax.fori_loop(0, 3, inner_middles, 0)
     lax.fori_loop(0, 3, quick_middles, 0)
 
+    shared = [[slow_unit(j, e) for e in range(frames - j)] for j in range(SHARED)]
+    bases = [3 * (INNER + QUICK) + sum(map(len, shared[:j])) for j in range(SHARED)]
+    for j, base in enumerate(bases):
+
+        @if_slow
+        def _(j=j):
+            take_near(slow, j)
+
+        middles(shared[j], base)
+
+    @if_slow
+    def _():
+        back_copy(slow, SHARED, pl.ds(HMAX, depth - EDGE)).start()
+
     waiter(edge_in, edge_send, edge_recv).wait_recv()
     halo_copy().start()
     for f in range(frames):
@@ -483,27 +504,23 @@
             put_edges(2 * f + s, edge_in[0, f, :, lanes], edge_in[1, f, :, lanes])
 
     edge_window = edge_band[...].astype(jnp.bfloat16)
-    lax.fori_loop(0, 3, inner_rims, 0)
-
-    for j in range(SHARED):
-
-        @if_slow
-        def _(j=j):
-            if j == 0:
-                take_far(slow)
-            take_near(slow, j)
-
-        wholes([slow_unit(j, e) for e in range(frames - j)])
-
-        @if_slow
-        def _(j=j):
-            back_copy(slow, j, 1).start()
-
-    lax.fori_loop(0, 2, last_step, 0)
+
+    @if_slow
+    def _():
+        take_far(slow)
+
+    for j, base in enumerate(bases):
+        rims(shared[j], base)
+
+    @if_slow
+    def _():
+        for at in (0, depth - HMAX):
+            back_copy(slow, SHARED, pl.ds(at, HMAX)).start()
+
     take_far(quick)
     lax.fori_loop(0, 3, quick_rims, 0)
-    back_copy(quick, 0, frames).start()
-    lax.fori_loop(2, 4, last_step, 0)
+    back_copy(quick, frames, pl.ds(0, depth)).start()
+    lax.fori_loop(0, 3, inner_rims, 0)
 
     frame_total = frames * blocks
 
@@ -526,8 +543,10 @@
 
         lax.fori_loop(0, frames, write_frame, 0)
 
+    lax.fori_loop(0, 2, last_step, 0)
     waiter(back.at[quick], back_send.at[quick], back_recv.at[quick]).wait()
     write(quick)
+    lax.fori_loop(2, 4, last_step, 0)
 
     @if_slow
     def _():
@@ -574,7 +593,7 @@
             pltpu.VMEM((slots, 2, depth, strip), wide),
             pltpu.VMEM((slots, 2, EDGE, strip), wide),
             pltpu.VMEM((slots, depth, strip), wide),
-            pltpu.VMEM((3 * (INNER + QUICK), 2, EDGE, strip), wide),
+            pltpu.VMEM((3 * (INNER + QUICK) + SHARED_STRIPS, 2, EDGE, strip), wide),
             pltpu.VMEM((2 * depth, 4 * (depth + EDGE)), wide),
             pltpu.VMEM((8 * EDGE, 16 * EDGE), wide),
             pltpu.VMEM((2, frames, depth, strip), wide),

time: 18.4 us -> 18.7 us (1.016)
  Pallas kernels: 17.5 us -> 17.8 us
    pallas_call x1, Pallas kernels: 17.5 us -> 17.8 us  [shards(): pl.pallas_call(kernel, out_shape=pltpu.VMEM((frames, depth, lines), wide)...]
where the time goes in v6:
time: 18.7 us; the launch traced here: 18.6 us
  Pallas kernels  17.8 us (95%)
  local copies, waits for them, and re-layouts  0.82 us (4%)
    pallas_call x1, Pallas kernels, shards(): pl.pallas_call(kernel, out_shape=pltpu.VMEM((frames, depth, lines), wide)...  17.8 us
    unnamed x1, local copies, waits for them, and re-layouts  0.82 us

profile of v6, /device:TPU:103, one launch (start us, length us, event | category | flops | bytes accessed | tf_op | source)
XLA Modules:
  0.0 18.6 jit_solution(16822038828835553593)
XLA Ops:
  0.0 17.8 %pair_phases.1 = f32[6,48,512]{2,1,0:T(8,128)S(1)} custom-call(bf16[2,6,48,512]{3,2,1,0:T(8,128)(2,1)} %iq_any.1, s32[48]{0:T(128)} %half_any.1, s32[6]{0:T(128)} %weights_any.1), custom_call_target="tpu_custom_call" | custom-call | tf_op jit(solution)/shard_map/pair_phases/pallas_call | solution.py:577
  17.8 0.8 %copy.5 = f32[6,48,512]{2,1,0:T(8,128)} copy(f32[6,48,512]{2,1,0:T(8,128)S(1)} %pair_phases.1) | data formatting | bytes 1179648

commit v7 on v6

--- a/solution.py
+++ b/solution.py
@@ -63,7 +63,7 @@
     iq_any, half_any, weights_any, out,
     half, weights, scaled, own16, edge_out, edge_in, near16, near_edge, more16, more_edge,
     field, edges, total, held, band, edge_band, back,
-    load_sem, small_sem, edge_send, edge_recv, near_send, near_recv, far_send, far_recv,
+    load_sem, small_sem, edge_send, edge_recv, near_send, near_recv, far_send, far_recv, halo_send, halo_recv,
     more_send, more_recv, rest_send, rest_recv, back_send, back_recv,
 ):
     frames, depth, lines = own16.shape[1:]
@@ -75,6 +75,7 @@
     slow = lax.rem(me, 2)
     quick = 1 - slow
     beside = (me > 0, me < blocks - 1)
+    slab_at = (level > 0, level < slabs - 1)
     target = me - 1 + 2 * slow
     slow_here = (target >= 0) & (target < blocks)
 
@@ -87,13 +88,22 @@
     for copy in small:
         copy.start()
     barrier = pltpu.get_barrier_semaphore()
-    for other in (below, above):
-        pl.semaphore_signal(barrier, inc=1, device_id=(me, other), device_id_type=MESH)
+    for way, other in enumerate((below, above)):
+
+        @pl.when(slab_at[way])
+        def _(other=other):
+            pl.semaphore_signal(barrier, inc=1, device_id=(me, other), device_id_type=MESH)
+
     for side, column in enumerate((left, right)):
 
         @pl.when(beside[side])
         def _(column=column):
-            for other in (level, below, above):
+            pl.semaphore_signal(barrier, inc=1, device_id=(column, level), device_id_type=MESH)
+
+        for way, other in enumerate((below, above)):
+
+            @pl.when(beside[side] & slab_at[way])
+            def _(column=column, other=other):
                 pl.semaphore_signal(barrier, inc=1, device_id=(column, other), device_id_type=MESH)
 
     def cut(side):
@@ -109,8 +119,8 @@
         return pltpu.make_async_remote_copy(
             src_ref=edge_out.at[way],
             dst_ref=edge_in.at[1 - way],
-            send_sem=edge_send,
-            recv_sem=edge_recv,
+            send_sem=edge_send.at[way],
+            recv_sem=edge_recv.at[1 - way],
             device_id=(me, below if way == 0 else above),
             device_id_type=MESH,
         )
@@ -129,8 +139,8 @@
         return pltpu.make_async_remote_copy(
             src_ref=edge_out.at[way, :, :, cut(slow)],
             dst_ref=near_edge.at[1 - slow, 1 - way],
-            send_sem=far_send.at[slow],
-            recv_sem=far_recv.at[1 - slow],
+            send_sem=far_send.at[way],
+            recv_sem=far_recv.at[1 - way],
             device_id=(next_to(slow), below if way == 0 else above),
             device_id_type=MESH,
         )
@@ -149,8 +159,8 @@
         return pltpu.make_async_remote_copy(
             src_ref=edge_out.at[way, pl.ds(slow * (frames - SHARED), SHARED), :, cut(quick)],
             dst_ref=more_edge.at[1 - way],
-            send_sem=rest_send,
-            recv_sem=rest_recv,
+            send_sem=rest_send.at[way],
+            recv_sem=rest_recv.at[1 - way],
             device_id=(next_to(slow), below if way == 0 else above),
             device_id_type=MESH,
         )
@@ -159,8 +169,8 @@
         return pltpu.make_async_remote_copy(
             src_ref=edge_in.at[:, :, :, cut(quick)],
             dst_ref=near_edge.at[1 - quick],
-            send_sem=far_send.at[quick],
-            recv_sem=far_recv.at[1 - quick],
+            send_sem=halo_send,
+            recv_sem=halo_recv,
             device_id=(next_to(quick), level),
             device_id_type=MESH,
         )
@@ -186,7 +196,9 @@
         pl.when(slow_here)(act)
 
     total[...] = jnp.zeros_like(total)
-    pl.semaphore_wait(barrier, 2 + 3 * sum(side.astype(jnp.int32) for side in beside))
+    columns = sum(here.astype(jnp.int32) for here in beside)
+    others = sum(here.astype(jnp.int32) for here in slab_at)
+    pl.semaphore_wait(barrier, others + columns * (1 + others))
 
     @if_slow
     def _():
@@ -205,20 +217,38 @@
         edge_out[1, f] = jnp.concatenate(last, axis=0).astype(jnp.bfloat16)
 
 
-    @if_slow
-    def _():
-        for way in range(2):
+    for way in range(2):
+
+        @pl.when(slow_here & slab_at[way])
+        def _(way=way):
             far_copy(way).start()
 
+
     for way in range(2):
-        edge_copy(way).start()
+
+        @pl.when(slab_at[way])
+        def _(way=way):
+            edge_copy(way).start()
+
+        @pl.when(jnp.logical_not(slab_at[way]))
+        def _(way=way):
+            edge_in[way] = jnp.zeros(edge_in.shape[1:], jnp.bfloat16)
+            near_edge[slow, way] = jnp.zeros(near_edge.shape[2:], jnp.bfloat16)
+            more_edge[way] = jnp.zeros(more_edge.shape[1:], jnp.bfloat16)
 
     @if_slow
     def _():
         for j in range(SHARED, frames):
             near_copy(slow, j).start()
-        for way in range(2):
+
+    for way in range(2):
+
+        @pl.when(slow_here & slab_at[way])
+        def _(way=way):
             rest_copy(way).start()
+
+    @if_slow
+    def _():
         for j in range(SHARED):
             more_copy(j).start()
 
@@ -284,8 +314,21 @@
             wide = near16[side, j, c].astype(jnp.float32) * 0.5
             field[2 * frames + frames * side + j, c] = wide
 
+    def wait_ways(refs, send, recv):
+        for way in range(2):
+
+            @pl.when(slab_at[way])
+            def _(way=way):
+                waiter(refs.at[way], send.at[way], recv.at[way]).wait_recv()
+
+    def sent_ways(refs, send):
+        for way in range(2):
+
+            @pl.when(slab_at[way])
+            def _(way=way):
+                waiter(refs.at[way], send.at[way], send.at[way]).wait_send()
+
     def take_far(side):
-        waiter(near_edge.at[side], far_send.at[side], far_recv.at[side]).wait_recv()
         for j in range(frames):
             frame = frame_at(1 - side, j)
             slot = 2 * frames + frames * side + j
@@ -297,7 +340,7 @@
             field[4 * frames + j, c] = more16[j, c].astype(jnp.float32) * 0.5
 
     def take_rest():
-        waiter(more_edge, rest_send, rest_recv).wait_recv()
+        wait_ways(more_edge, rest_send, rest_recv)
         for j in range(SHARED):
             k = SHARED - 1 - j + slow * (2 * j - SHARED + 1)
             put_edges(4 * frames + j, more_edge[0, k], more_edge[1, k])
@@ -496,7 +539,7 @@
     def _():
         back_copy(slow, SHARED, pl.ds(HMAX, depth - EDGE)).start()
 
-    waiter(edge_in, edge_send, edge_recv).wait_recv()
+    wait_ways(edge_in, edge_send, edge_recv)
     halo_copy().start()
     for f in range(frames):
         for s in range(2):
@@ -507,6 +550,7 @@
 
     @if_slow
     def _():
+        wait_ways(near_edge.at[slow], far_send, far_recv)
         take_far(slow)
 
     for j, base in enumerate(bases):
@@ -517,6 +561,7 @@
         for at in (0, depth - HMAX):
             back_copy(slow, SHARED, pl.ds(at, HMAX)).start()
 
+    waiter(near_edge.at[quick], halo_send, halo_recv).wait_recv()
     take_far(quick)
     lax.fori_loop(0, 3, quick_rims, 0)
     back_copy(quick, frames, pl.ds(0, depth)).start()
@@ -556,16 +601,14 @@
 
     @if_slow
     def _():
-        waiter(more_edge, rest_send, rest_recv).wait_send()
+        sent_ways(more_edge, rest_send)
+        sent_ways(near_edge.at[slow], far_send)
         waiter(more16, more_send, more_send).wait_send()
-
-    waiter(edge_out, edge_send, edge_recv).wait_send()
-    for side, here in ((quick, True), (slow, slow_here)):
-
-        @pl.when(here)
-        def _(side=side):
-            waiter(near_edge.at[side], far_send.at[side], far_recv.at[side]).wait_send()
-            waiter(near16.at[side], near_send.at[side], near_send.at[side]).wait_send()
+        waiter(near16.at[slow], near_send.at[slow], near_send.at[slow]).wait_send()
+
+    sent_ways(edge_out, edge_send)
+    waiter(near_edge.at[quick], halo_send, halo_send).wait_send()
+    waiter(near16.at[quick], near_send.at[quick], near_send.at[quick]).wait_send()
 
 
 def shards(iq, half, weights):
@@ -599,16 +642,18 @@
             pltpu.VMEM((2, frames, depth, strip), wide),
             dma(()),
             dma((2,)),
+            dma((2,)),
+            dma((2,)),
+            dma((2,)),
+            dma((2, frames)),
+            dma((2,)),
+            dma((2,)),
             dma(()),
             dma(()),
-            dma((2,)),
-            dma((2, frames)),
-            dma((2,)),
-            dma((2,)),
             dma(()),
             dma((SHARED,)),
-            dma(()),
-            dma(()),
+            dma((2,)),
+            dma((2,)),
             dma((2,)),
             dma((2,)),
         ],

time: 18.7 us -> 17.8 us (0.952)
  Pallas kernels: 17.8 us -> 16.9 us
    pallas_call x1, Pallas kernels: 17.8 us -> 16.9 us  [shards(): pl.pallas_call(kernel, out_shape=pltpu.VMEM((frames, depth, lines), wide)...]
where the time goes in v7:
time: 17.8 us; the launch traced here: 17.7 us
  Pallas kernels  16.9 us (95%)
  local copies, waits for them, and re-layouts  0.82 us (5%)
    pallas_call x1, Pallas kernels, shards(): pl.pallas_call(kernel, out_shape=pltpu.VMEM((frames, depth, lines), wide)...  16.9 us
    unnamed x1, local copies, waits for them, and re-layouts  0.82 us

profile of v7, /device:TPU:103, one launch (start us, length us, event | category | flops | bytes accessed | tf_op | source)
XLA Modules:
  0.0 17.7 jit_solution(4033664982053554326)
XLA Ops:
  0.0 16.9 %pair_phases.1 = f32[6,48,512]{2,1,0:T(8,128)S(1)} custom-call(bf16[2,6,48,512]{3,2,1,0:T(8,128)(2,1)} %iq_any.1, s32[48]{0:T(128)} %half_any.1, s32[6]{0:T(128)} %weights_any.1), custom_call_target="tpu_custom_call" | custom-call | tf_op jit(solution)/shard_map/pair_phases/pallas_call | solution.py:620
  16.9 0.8 %copy.5 = f32[6,48,512]{2,1,0:T(8,128)} copy(f32[6,48,512]{2,1,0:T(8,128)S(1)} %pair_phases.1) | data formatting | bytes 1179648

commit v8 on v7

--- a/solution.py
+++ b/solution.py
@@ -135,12 +135,15 @@
             device_id_type=MESH,
         )
 
-    def far_copy(way):
-        return pltpu.make_async_remote_copy(
-            src_ref=edge_out.at[way, :, :, cut(slow)],
-            dst_ref=near_edge.at[1 - slow, 1 - way],
-            send_sem=far_send.at[way],
-            recv_sem=far_recv.at[1 - way],
+    def part_of(side, part):
+        return pl.ds((side + part - 2 * side * part) * SHARED, SHARED)
+
+    def far_copy(way, part):
+        return pltpu.make_async_remote_copy(
+            src_ref=edge_out.at[way, part_of(slow, part), :, cut(slow)],
+            dst_ref=near_edge.at[1 - slow, 1 - way, part_of(slow, part)],
+            send_sem=far_send.at[part, way],
+            recv_sem=far_recv.at[part, 1 - way],
             device_id=(next_to(slow), below if way == 0 else above),
             device_id_type=MESH,
         )
@@ -221,7 +224,7 @@
 
         @pl.when(slow_here & slab_at[way])
         def _(way=way):
-            far_copy(way).start()
+            far_copy(way, 0).start()
 
 
     for way in range(2):
@@ -245,6 +248,7 @@
 
         @pl.when(slow_here & slab_at[way])
         def _(way=way):
+            far_copy(way, 1).start()
             rest_copy(way).start()
 
     @if_slow
@@ -328,8 +332,16 @@
             def _(way=way):
                 waiter(refs.at[way], send.at[way], send.at[way]).wait_send()
 
-    def take_far(side):
-        for j in range(frames):
+    def wait_far(part):
+        for way in range(2):
+
+            @pl.when(slab_at[way])
+            def _(way=way):
+                ref = near_edge.at[slow, way, part_of(quick, part)]
+                waiter(ref, far_send.at[part, way], far_recv.at[part, way]).wait_recv()
+
+    def take_far(side, first, count):
+        for j in range(first, first + count):
             frame = frame_at(1 - side, j)
             slot = 2 * frames + frames * side + j
             put_edges(slot, near_edge[side, 0, frame], near_edge[side, 1, frame])
@@ -489,6 +501,8 @@
     def last_step(n, carry):
         @pl.when((n == 0) & slow_here)
         def _():
+            wait_far(1)
+            take_far(slow, SHARED, SHARED)
             take_near(slow, 3)
 
         @pl.when((n == 1) & slow_here)
@@ -550,8 +564,8 @@
 
     @if_slow
     def _():
-        wait_ways(near_edge.at[slow], far_send, far_recv)
-        take_far(slow)
+        wait_far(0)
+        take_far(slow, 0, SHARED)
 
     for j, base in enumerate(bases):
         rims(shared[j], base)
@@ -562,7 +576,7 @@
             back_copy(slow, SHARED, pl.ds(at, HMAX)).start()
 
     waiter(near_edge.at[quick], halo_send, halo_recv).wait_recv()
-    take_far(quick)
+    take_far(quick, 0, frames)
     lax.fori_loop(0, 3, quick_rims, 0)
     back_copy(quick, frames, pl.ds(0, depth)).start()
     lax.fori_loop(0, 3, inner_rims, 0)
@@ -602,7 +616,8 @@
     @if_slow
     def _():
         sent_ways(more_edge, rest_send)
-        sent_ways(near_edge.at[slow], far_send)
+        for part in range(2):
+            sent_ways(near_edge.at[slow, :, part_of(slow, part)], far_send.at[part])
         waiter(more16, more_send, more_send).wait_send()
         waiter(near16.at[slow], near_send.at[slow], near_send.at[slow]).wait_send()
 
@@ -646,8 +661,8 @@
             dma((2,)),
             dma((2,)),
             dma((2, frames)),
-            dma((2,)),
-            dma((2,)),
+            dma((2, 2)),
+            dma((2, 2)),
             dma(()),
             dma(()),
             dma(()),

time: 17.8 us -> 17.4 us (0.978)
  Pallas kernels: 16.9 us -> 16.5 us
    pallas_call x1, Pallas kernels: 16.9 us -> 16.5 us  [shards(): pl.pallas_call(kernel, out_shape=pltpu.VMEM((frames, depth, lines), wide)...]
where the time goes in v8:
time: 17.4 us; the launch traced here: 17.3 us
  Pallas kernels  16.5 us (95%)
  local copies, waits for them, and re-layouts  0.82 us (5%)
    pallas_call x1, Pallas kernels, shards(): pl.pallas_call(kernel, out_shape=pltpu.VMEM((frames, depth, lines), wide)...  16.5 us
    unnamed x1, local copies, waits for them, and re-layouts  0.82 us

profile of v8, /device:TPU:103, one launch (start us, length us, event | category | flops | bytes accessed | tf_op | source)
XLA Modules:
  0.0 17.3 jit_solution(11613428655983416237)
XLA Ops:
  0.0 16.5 %pair_phases.1 = f32[6,48,512]{2,1,0:T(8,128)S(1)} custom-call(bf16[2,6,48,512]{3,2,1,0:T(8,128)(2,1)} %iq_any.1, s32[48]{0:T(128)} %half_any.1, s32[6]{0:T(128)} %weights_any.1), custom_call_target="tpu_custom_call" | custom-call | tf_op jit(solution)/shard_map/pair_phases/pallas_call | solution.py:635
  16.5 0.8 %copy.5 = f32[6,48,512]{2,1,0:T(8,128)} copy(f32[6,48,512]{2,1,0:T(8,128)S(1)} %pair_phases.1) | data formatting | bytes 1179648

commit v9 on v8

--- a/solution.py
+++ b/solution.py
@@ -205,7 +205,7 @@
 
     @if_slow
     def _():
-        for j in range(SHARED):
+        for j in range(2):
             near_copy(slow, j).start()
 
     load.wait()
@@ -241,7 +241,7 @@
 
     @if_slow
     def _():
-        for j in range(SHARED, frames):
+        for j in range(2, frames):
             near_copy(slow, j).start()
 
     for way in range(2):
@@ -567,8 +567,7 @@
         wait_far(0)
         take_far(slow, 0, SHARED)
 
-    for j, base in enumerate(bases):
-        rims(shared[j], base)
+    rims(sum(shared, []), bases[0])
 
     @if_slow
     def _():

time: 17.4 us -> 17.6 us (1.011)
  the two profiles are of different devices: /device:TPU:103 before, /device:TPU:111 now
where the time goes in v9:
time: 17.6 us; the launch traced here: 17.5 us
  Pallas kernels  16.7 us (95%)
  local copies, waits for them, and re-layouts  0.82 us (5%)
    pallas_call x1, Pallas kernels, shards(): pl.pallas_call(kernel, out_shape=pltpu.VMEM((frames, depth, lines), wide)...  16.7 us
    unnamed x1, local copies, waits for them, and re-layouts  0.82 us

profile of v9, /device:TPU:111, one launch (start us, length us, event | category | flops | bytes accessed | tf_op | source)
XLA Modules:
  0.0 17.5 jit_solution(13279411858776199162)
XLA Ops:
  0.0 16.7 %pair_phases.1 = f32[6,48,512]{2,1,0:T(8,128)S(1)} custom-call(bf16[2,6,48,512]{3,2,1,0:T(8,128)(2,1)} %iq_any.1, s32[48]{0:T(128)} %half_any.1, s32[6]{0:T(128)} %weights_any.1), custom_call_target="tpu_custom_call" | custom-call | tf_op jit(solution)/shard_map/pair_phases/pallas_call | solution.py:634
  16.7 0.8 %copy.5 = f32[6,48,512]{2,1,0:T(8,128)} copy(f32[6,48,512]{2,1,0:T(8,128)S(1)} %pair_phases.1) | data formatting | bytes 1179648

commit v10 on v8

--- a/solution.py
+++ b/solution.py
@@ -567,8 +567,7 @@
         wait_far(0)
         take_far(slow, 0, SHARED)
 
-    for j, base in enumerate(bases):
-        rims(shared[j], base)
+    rims(sum(shared, []), bases[0])
 
     @if_slow
     def _():

time: 17.4 us -> 17.4 us (level)
  no operation moved by 1% of the time
where the time goes in v10:
time: 17.4 us; the launch traced here: 17.3 us
  Pallas kernels  16.5 us (95%)
  local copies, waits for them, and re-layouts  0.82 us (5%)
    pallas_call x1, Pallas kernels, shards(): pl.pallas_call(kernel, out_shape=pltpu.VMEM((frames, depth, lines), wide)...  16.5 us
    unnamed x1, local copies, waits for them, and re-layouts  0.82 us

profile of v10, /device:TPU:103, one launch (start us, length us, event | category | flops | bytes accessed | tf_op | source)
XLA Modules:
  0.0 17.3 jit_solution(15185852700459137323)
XLA Ops:
  0.0 16.5 %pair_phases.1 = f32[6,48,512]{2,1,0:T(8,128)S(1)} custom-call(bf16[2,6,48,512]{3,2,1,0:T(8,128)(2,1)} %iq_any.1, s32[48]{0:T(128)} %half_any.1, s32[6]{0:T(128)} %weights_any.1), custom_call_target="tpu_custom_call" | custom-call | tf_op jit(solution)/shard_map/pair_phases/pallas_call | solution.py:634
  16.5 0.8 %copy.5 = f32[6,48,512]{2,1,0:T(8,128)} copy(f32[6,48,512]{2,1,0:T(8,128)S(1)} %pair_phases.1) | data formatting | bytes 1179648

commit v11 on v8

--- a/solution.py
+++ b/solution.py
@@ -600,7 +600,8 @@
                 out[f, part, lanes] = (total[slot, part] + back[side, j, part]) * inverse
             return carry
 
-        lax.fori_loop(0, frames, write_frame, 0)
+        for f in range(frames):
+            write_frame(f, 0)
 
     lax.fori_loop(0, 2, last_step, 0)
     waiter(back.at[quick], back_send.at[quick], back_recv.at[quick]).wait()

time: 17.4 us -> 17.3 us (level)
  no operation moved by 1% of the time
where the time goes in v11:
time: 17.3 us; the launch traced here: 17.2 us
  Pallas kernels  16.4 us (95%)
  local copies, waits for them, and re-layouts  0.82 us (5%)
    pallas_call x1, Pallas kernels, shards(): pl.pallas_call(kernel, out_shape=pltpu.VMEM((frames, depth, lines), wide)...  16.4 us
    unnamed x1, local copies, waits for them, and re-layouts  0.82 us

profile of v11, /device:TPU:103, one launch (start us, length us, event | category | flops | bytes accessed | tf_op | source)
XLA Modules:
  0.0 17.2 jit_solution(16632191096829505200)
XLA Ops:
  0.0 16.4 %pair_phases.1 = f32[6,48,512]{2,1,0:T(8,128)S(1)} custom-call(bf16[2,6,48,512]{3,2,1,0:T(8,128)(2,1)} %iq_any.1, s32[48]{0:T(128)} %half_any.1, s32[6]{0:T(128)} %weights_any.1), custom_call_target="tpu_custom_call" | custom-call | tf_op jit(solution)/shard_map/pair_phases/pallas_call | solution.py:636
  16.4 0.8 %copy.5 = f32[6,48,512]{2,1,0:T(8,128)} copy(f32[6,48,512]{2,1,0:T(8,128)S(1)} %pair_phases.1) | data formatting | bytes 1179648
